TPU v7x, 32 devices: a whole 2x2x4 slice. The times are simulated.
32 devices in a mesh: seq: 8 (over y, x, core), rows: 4 (over z).
Axes of the slice: x: 2, y: 2, z: 4, core: 2. Of those that a mesh axis runs over, the one named last changes fastest.
Arguments:
- queries: bfloat16 [24, 2048, 768], P('rows', 'seq'), may hold values from -6 to 6
- latents: bfloat16 [24, 256, 1280], P('rows', 'seq'), may hold values from -6 to 6
- query_ids: int32 [24, 2048], P('rows', 'seq'), may hold values from 0 to 3, as said below
- latent_ids: int32 [24, 256], P('rows'), may hold values from 0 to 3, as said below
- query_weight: bfloat16 [768, 256], replicated, may hold values from -0.21875 to 0.21875
- key_weight: bfloat16 [1280, 256], replicated, may hold values from -0.15625 to 0.15625
- value_weight: bfloat16 [1280, 768], replicated, may hold values from -0.15625 to 0.15625
- out_weight: bfloat16 [768, 768], replicated, may hold values from -1.75 to 1.75
- up_weight: bfloat16 [768, 768], replicated, may hold values from -0.21875 to 0.21875
- down_weight: bfloat16 [768, 768], replicated, may hold values from -0.21875 to 0.21875
- gain_query: float32 [768], replicated, may hold values from 0.1 to 1.9
- shift_query: float32 [768], replicated, may hold values from -3 to 3
- gain_latent: float32 [1280], replicated, may hold values from 0.1 to 1.9
- shift_latent: float32 [1280], replicated, may hold values from -3 to 3
- gain_hidden: float32 [768], replicated, may hold values from 0.1 to 1.9
- shift_hidden: float32 [768], replicated, may hold values from -3 to 3
- bias_up: float32 [768], replicated, may hold values from -3 to 3
- bias_down: float32 [768], replicated, may hold values from -3 to 3
- cotangent: bfloat16 [24, 2048, 768], P('rows', 'seq'), may hold values from -6 to 6
Outputs:
- block_out: bfloat16 [24, 2048, 768], P('rows', 'seq')
- grad_queries: float32 [24, 2048, 768], P('rows', 'seq')
- grad_latents: float32 [24, 256, 1280], P('rows', 'seq')
- grad_query_weight: float32 [768, 256], P('seq')
- grad_key_weight: float32 [1280, 256], P('seq')
- grad_value_weight: float32 [1280, 768], P('seq')
- grad_out_weight: float32 [768, 768], P('seq')
- grad_up_weight: float32 [768, 768], P('seq')
- grad_down_weight: float32 [768, 768], P('seq')
- grad_gain_query: float32 [768], P('seq')
- grad_shift_query: float32 [768], P('seq')
- grad_gain_latent: float32 [1280], P('seq')
- grad_shift_latent: float32 [1280], P('seq')
- grad_gain_hidden: float32 [768], P('seq')
- grad_shift_hidden: float32 [768], P('seq')
- grad_bias_up: float32 [768], P('seq')
- grad_bias_down: float32 [768], P('seq')
Inputs may be any that keep to these rules, and one draw needn't show every extreme that they name: `query_ids`: within each row the ids never fall, start at 0 and take every value up to 3. `latent_ids`: in each row, every aligned block of 32 latents holds every id of 0 to 3 at least once.
All inputs are finite; a program needn't handle non-finite values.
Results may differ from a plain program's by a relative error of at most 0.015.
Values may be sent and summed in bfloat16 or wider, within the bound.
A program may use at most 128 MiB of HBM per device.

v0:
```python
import jax
import jax.numpy as jnp
from jax import lax
from jax.sharding import PartitionSpec as P

HEADS = 8
HDIM = 96
QKDIM = 32


EPS = 1e-05


def normalize(field):
    center = field - jnp.mean(field, axis=-1, keepdims=True)
    inverse = lax.rsqrt(jnp.mean(center * center, axis=-1, keepdims=True) + EPS)
    return (center * inverse, inverse)


def norm_back(grad, gain, normed_hat, inverse):
    scaled = grad * gain
    return inverse * (
        scaled
        - jnp.mean(scaled, axis=-1, keepdims=True)
        - normed_hat * jnp.mean(scaled * normed_hat, axis=-1, keepdims=True)
    )


def weight_grad(left, right):
    return jnp.einsum("rqi,rqj->ij", left, right, preferred_element_type=jnp.float32)


def input_grad(grad, weight):
    return jnp.einsum("rqj,ij->rqi", grad, weight, preferred_element_type=jnp.float32)


def total_sum(field):
    return jnp.sum(field, axis=(0, 1))


def masked_scores(heads_query, heads_key, allowed):
    scores = jnp.einsum(
        "rqhd,rkhd->rhqk", heads_query, heads_key, preferred_element_type=jnp.float32
    )
    return jnp.where(allowed[:, None], scores, -1e30)


def body(
    queries,
    latents,
    query_ids,
    latent_ids,
    query_weight,
    key_weight,
    value_weight,
    out_weight,
    up_weight,
    down_weight,
    gain_query,
    shift_query,
    gain_latent,
    shift_latent,
    gain_hidden,
    shift_hidden,
    bias_up,
    bias_down,
    cotangent,
):
    rows_here, positions, width = queries.shape
    scale = QKDIM ** (-0.5)
    query_full = queries.astype(jnp.float32)
    query_hat, query_inv = normalize(query_full)
    query_normed = (query_hat * gain_query + shift_query).astype(jnp.bfloat16)
    query_proj = (
        jnp.dot(query_normed, query_weight, preferred_element_type=jnp.float32) * scale
    ).astype(jnp.bfloat16)
    latent_hat, latent_inv = normalize(latents.astype(jnp.float32))
    latent_normed = (latent_hat * gain_latent + shift_latent).astype(jnp.bfloat16)
    own_keys = jnp.dot(latent_normed, key_weight, preferred_element_type=jnp.float32).astype(
        jnp.bfloat16
    )
    own_values = jnp.dot(latent_normed, value_weight, preferred_element_type=jnp.float32).astype(
        jnp.bfloat16
    )
    key_all, value_all = (
        lax.all_gather(own_keys, "seq", axis=1, tiled=True),
        lax.all_gather(own_values, "seq", axis=1, tiled=True),
    )
    allowed = query_ids[:, :, None] == latent_ids[:, None, :]
    heads_query = query_proj.reshape(rows_here, positions, HEADS, QKDIM)
    heads_key = key_all.reshape(rows_here, -1, HEADS, QKDIM)
    heads_value = value_all.reshape(rows_here, -1, HEADS, HDIM)
    scores = masked_scores(heads_query, heads_key, allowed)
    row_top = jnp.max(scores, axis=-1, keepdims=True)
    unscaled = jnp.exp(scores - row_top)
    row_total = jnp.sum(unscaled, axis=-1, keepdims=True)
    log_total = row_top + jnp.log(row_total)
    probs_low = (unscaled / row_total).astype(jnp.bfloat16)
    mixed = jnp.einsum(
        "rhqk,rkhd->rqhd", probs_low, heads_value, preferred_element_type=jnp.float32
    )
    mixed = mixed.reshape(rows_here, positions, width).astype(jnp.bfloat16)
    resid = query_full + jnp.dot(mixed, out_weight, preferred_element_type=jnp.float32)
    hidden_hat, hidden_inv = normalize(resid)
    hidden_normed = (hidden_hat * gain_hidden + shift_hidden).astype(jnp.bfloat16)
    pre = jnp.dot(hidden_normed, up_weight, preferred_element_type=jnp.float32) + bias_up
    act_value, gelu_pull = jax.vjp(lambda field: jax.nn.gelu(field, approximate=False), pre)
    act = act_value.astype(jnp.bfloat16)
    block_out = (
        resid + jnp.dot(act, down_weight, preferred_element_type=jnp.float32) + bias_down
    ).astype(jnp.bfloat16)
    cot_full = cotangent.astype(jnp.float32)
    grad_bias_down = total_sum(cot_full)
    grad_down_weight = weight_grad(act, cotangent)
    d_act = input_grad(cotangent, down_weight)
    d_pre = gelu_pull(d_act)[0].astype(jnp.bfloat16)
    grad_bias_up = total_sum(d_pre.astype(jnp.float32))
    grad_up_weight = weight_grad(hidden_normed, d_pre)
    d_hidden = input_grad(d_pre, up_weight)
    grad_gain_hidden = total_sum(d_hidden * hidden_hat)
    grad_shift_hidden = total_sum(d_hidden)
    d_resid = norm_back(d_hidden, gain_hidden, hidden_hat, hidden_inv) + cot_full
    d_resid_low = d_resid.astype(jnp.bfloat16)
    grad_out_weight = weight_grad(mixed, d_resid_low)
    d_mixed = input_grad(d_resid_low, out_weight).astype(jnp.bfloat16)
    heads_dmixed = d_mixed.reshape(rows_here, positions, HEADS, HDIM)
    probs_again = jnp.exp(masked_scores(heads_query, heads_key, allowed) - log_total)
    probs_again_low = probs_again.astype(jnp.bfloat16)
    d_probs = jnp.einsum(
        "rqhd,rkhd->rhqk", heads_dmixed, heads_value, preferred_element_type=jnp.float32
    )
    row_delta = jnp.sum(probs_again * d_probs, axis=-1, keepdims=True)
    d_scores = (probs_again * (d_probs - row_delta)).astype(jnp.bfloat16)
    d_query = jnp.einsum("rhqk,rkhd->rqhd", d_scores, heads_key, preferred_element_type=jnp.float32)
    d_query = d_query.reshape(rows_here, positions, -1).astype(jnp.bfloat16)
    key_part = jnp.einsum(
        "rhqk,rqhd->rkhd", d_scores, heads_query, preferred_element_type=jnp.float32
    )
    value_part = jnp.einsum(
        "rhqk,rqhd->rkhd", probs_again_low, heads_dmixed, preferred_element_type=jnp.float32
    )
    key_part = key_part.reshape(rows_here, key_part.shape[1], -1)
    value_part = value_part.reshape(rows_here, value_part.shape[1], -1)
    grad_query_weight = weight_grad(query_normed, d_query) * scale
    d_qnorm = input_grad(d_query, query_weight) * scale
    grad_gain_query = total_sum(d_qnorm * query_hat)
    grad_shift_query = total_sum(d_qnorm)
    grad_queries = norm_back(d_qnorm, gain_query, query_hat, query_inv) + d_resid
    d_keys, d_values = (
        lax.psum_scatter(
            key_part.astype(jnp.bfloat16), "seq", scatter_dimension=1, tiled=True
        ).astype(jnp.float32),
        lax.psum_scatter(
            value_part.astype(jnp.bfloat16), "seq", scatter_dimension=1, tiled=True
        ).astype(jnp.float32),
    )
    d_keys = d_keys.astype(jnp.bfloat16)
    d_values = d_values.astype(jnp.bfloat16)
    grad_key_weight = weight_grad(latent_normed, d_keys)
    grad_value_weight = weight_grad(latent_normed, d_values)
    d_lnorm = input_grad(d_keys, key_weight) + input_grad(d_values, value_weight)
    grad_gain_latent = total_sum(d_lnorm * latent_hat)
    grad_shift_latent = total_sum(d_lnorm)
    grad_latents = norm_back(d_lnorm, gain_latent, latent_hat, latent_inv)
    (
        g_query,
        g_key,
        g_value,
        g_out,
        g_up,
        g_down,
        g_gain_q,
        g_shift_q,
        g_gain_l,
        g_shift_l,
        g_gain_h,
        g_shift_h,
        g_bias_u,
        g_bias_d,
    ) = (
        lax.psum_scatter(grad_query_weight, ("seq", "rows"), scatter_dimension=0, tiled=True),
        lax.psum_scatter(grad_key_weight, ("seq", "rows"), scatter_dimension=0, tiled=True),
        lax.psum_scatter(grad_value_weight, ("seq", "rows"), scatter_dimension=0, tiled=True),
        lax.psum_scatter(grad_out_weight, ("seq", "rows"), scatter_dimension=0, tiled=True),
        lax.psum_scatter(grad_up_weight, ("seq", "rows"), scatter_dimension=0, tiled=True),
        lax.psum_scatter(grad_down_weight, ("seq", "rows"), scatter_dimension=0, tiled=True),
        lax.psum_scatter(grad_gain_query, ("seq", "rows"), scatter_dimension=0, tiled=True),
        lax.psum_scatter(grad_shift_query, ("seq", "rows"), scatter_dimension=0, tiled=True),
        lax.psum_scatter(grad_gain_latent, ("seq", "rows"), scatter_dimension=0, tiled=True),
        lax.psum_scatter(grad_shift_latent, ("seq", "rows"), scatter_dimension=0, tiled=True),
        lax.psum_scatter(grad_gain_hidden, ("seq", "rows"), scatter_dimension=0, tiled=True),
        lax.psum_scatter(grad_shift_hidden, ("seq", "rows"), scatter_dimension=0, tiled=True),
        lax.psum_scatter(grad_bias_up, ("seq", "rows"), scatter_dimension=0, tiled=True),
        lax.psum_scatter(grad_bias_down, ("seq", "rows"), scatter_dimension=0, tiled=True),
    )
    shards = (
        lax.all_gather(g_query.astype(jnp.bfloat16), "rows", axis=0, tiled=True).astype(
            g_query.dtype
        ),
        lax.all_gather(g_key.astype(jnp.bfloat16), "rows", axis=0, tiled=True).astype(g_key.dtype),
        lax.all_gather(g_value.astype(jnp.bfloat16), "rows", axis=0, tiled=True).astype(
            g_value.dtype
        ),
        lax.all_gather(g_out.astype(jnp.bfloat16), "rows", axis=0, tiled=True).astype(g_out.dtype),
        lax.all_gather(g_up.astype(jnp.bfloat16), "rows", axis=0, tiled=True).astype(g_up.dtype),
        lax.all_gather(g_down.astype(jnp.bfloat16), "rows", axis=0, tiled=True).astype(
            g_down.dtype
        ),
        lax.all_gather(g_gain_q.astype(jnp.bfloat16), "rows", axis=0, tiled=True).astype(
            g_gain_q.dtype
        ),
        lax.all_gather(g_shift_q.astype(jnp.bfloat16), "rows", axis=0, tiled=True).astype(
            g_shift_q.dtype
        ),
        lax.all_gather(g_gain_l.astype(jnp.bfloat16), "rows", axis=0, tiled=True).astype(
            g_gain_l.dtype
        ),
        lax.all_gather(g_shift_l.astype(jnp.bfloat16), "rows", axis=0, tiled=True).astype(
            g_shift_l.dtype
        ),
        lax.all_gather(g_gain_h.astype(jnp.bfloat16), "rows", axis=0, tiled=True).astype(
            g_gain_h.dtype
        ),
        lax.all_gather(g_shift_h.astype(jnp.bfloat16), "rows", axis=0, tiled=True).astype(
            g_shift_h.dtype
        ),
        lax.all_gather(g_bias_u.astype(jnp.bfloat16), "rows", axis=0, tiled=True).astype(
            g_bias_u.dtype
        ),
        lax.all_gather(g_bias_d.astype(jnp.bfloat16), "rows", axis=0, tiled=True).astype(
            g_bias_d.dtype
        ),
    )
    return (
        block_out,
        grad_queries,
        grad_latents,
        shards[0],
        shards[1],
        shards[2],
        shards[3],
        shards[4],
        shards[5],
        shards[6],
        shards[7],
        shards[8],
        shards[9],
        shards[10],
        shards[11],
        shards[12],
        shards[13],
    )


def solution(mesh):
    return jax.shard_map(
        body,
        mesh=mesh,
        in_specs=(
            P("rows", "seq", None),
            P("rows", "seq", None),
            P("rows", "seq"),
            P("rows", None),
            P(),
            P(),
            P(),
            P(),
            P(),
            P(),
            P(),
            P(),
            P(),
            P(),
            P(),
            P(),
            P(),
            P(),
            P("rows", "seq", None),
        ),
        out_specs=(
            P("rows", "seq", None),
            P("rows", "seq", None),
            P("rows", "seq", None),
            P("seq", None),
            P("seq", None),
            P("seq", None),
            P("seq", None),
            P("seq", None),
            P("seq", None),
            P("seq"),
            P("seq"),
            P("seq"),
            P("seq"),
            P("seq"),
            P("seq"),
            P("seq"),
            P("seq"),
        ),
        check_vma=False,
    )
```

profile of v0, /device:TPU:0, one launch (start us, length us, event | category | flops | bytes accessed | tf_op | source)
XLA Modules:
  0.0 889.5 jit_solution(6798772846531105510)
XLA Ops:
  12.9 13.0 %all_gather.49 = bf16[6,256,256]{2,1,0:T(8,128)(2,1)} all-gather(bf16[6,32,256]{2,1,0:T(8,128)(2,1)S(1)} %convolution_convert_fusion.3), channel_id=1, replica_groups=mesh['seq'=8,'rows'=4] {'seq'}, dimensions={1}, use_global_device_ids=true | all-gather | bytes 884736 | tf_op jit(solution)/shard_map/all_gather | solution.py:86
  49.0 8.5 fusion.28
  65.8 11.6 %multiply_convert_fusion.1 = (bf16[6,256,768]{2,1,0:T(8,128)(2,1)}, f32[6,256,768]{2,1,0:T(8,128)S(1)}) fusion(f32[6,256,768]{2,1,0:T(8,128)S(1)} %get-tuple-element.55, f32[768]{0:T(1024)S(1)} %copy-done.22, u8[256,768]{1,0:T(8,128)(4,1)S(1)} %get-tuple-element.24, u8[256,768]{1,0:T(8,128)(4,1)S(1)} %get-tuple-element.23), kind=kLoop, calls=%fused_computation.44 | loop fusion | flops 83755008 | bytes 12192768 | tf_op jit(solution)/shard_map/convert_element_type | solution.py:108
  96.7 13.8 %multiply_reduce_fusion = (f32[6,8,256]{2,1,0:T(8,128)S(1)}, f32[6,8,256,256]{2,3,1,0:T(8,128)}) fusion(f32[6,8,256,256]{2,3,1,0:T(8,128)} %copy-done.1, f32[6,8,256]{2,1,0:T(8,128)S(1)} %log_add_fusion, pred[6,256,256]{1,2,0:T(8,128)(4,1)S(1)} %broadcast_compare_fusion, bf16[6,256,8,96]{1,3,2,0:T(8,128)(2,1)} %bitcast.101, bf16[6,256,8,96]{1,3,2,0:T(8,128)(2,1)} %bitcast.108), kind=kOutput, calls=%fused_computation.1 | convolution fusion | flops 616550400 | bytes 30375936 | tf_op jit(solution)/shard_map/rqhd,rkhd->rhqk/dot_general | solution.py:129
  110.5 10.0 %multiply_convert_fusion = bf16[6,8,256,256]{2,3,1,0:T(8,128)(2,1)S(1)} fusion(f32[6,8,256,256]{2,3,1,0:T(8,128)} %get-tuple-element.58, f32[6,8,256,256]{2,3,1,0:T(8,128)} %copy-done.1, f32[6,8,256]{2,1,0:T(8,128)S(1)} %get-tuple-element.57, f32[6,8,256]{2,1,0:T(8,128)S(1)} %log_add_fusion, pred[6,256,256]{1,2,0:T(8,128)(4,1)S(1)} %broadcast_compare_fusion), kind=kLoop, calls=%fused_computation | loop fusion | flops 15728640 | bytes 31948800 | tf_op jit(solution)/shard_map/convert_element_type | solution.py:133
  128.3 9.4 %fusion.29 = bf16[6,8,96,256]{3,2,1,0:T(8,128)(2,1)} fusion(bf16[6,256,8,96]{1,3,2,0:T(8,128)(2,1)} %bitcast.102, f32[6,8,256,256]{2,3,1,0:T(8,128)} %copy-done.1, f32[6,8,256]{2,1,0:T(8,128)S(1)} %log_add_fusion, pred[6,256,256]{1,2,0:T(8,128)(4,1)S(1)} %broadcast_compare_fusion), kind=kOutput, calls=%fused_computation.67 | convolution fusion | flops 614596608 | bytes 17743872 | tf_op jit(solution)/shard_map/rhqk,rqhd->rkhd/dot_general | solution.py:139
  149.6 7.0 convolution_bitcast_fusion.3
  156.8 5.9 convolution_bitcast_fusion.2
  162.8 6.5 convolution_bitcast_fusion.4
  172.1 37.2 %reduce-scatter.11.cloned.1.call-done = bf16[6,32,768]{2,1,0:T(8,128)(2,1)} async-done(((bf16[6,256,768]{2,1,0:T(8,128)(2,1)}), bf16[6,32,768]{2,1,0:T(8,128)(2,1)}) %reduce-scatter.11.cloned.1.call-update) | async-done | bytes 294928 | tf_op jit(solution)/shard_map/reduce_scatter | solution.py:153
  226.5 84.0 %reduce-scatter.13.cloned.1.call-done = f32[24,256]{1,0:T(8,128)} async-done(((f32[768,256]{1,0:T(8,128)}), f32[24,256]{1,0:T(8,128)}) %reduce-scatter.13.cloned.1.call-update) | async-done | bytes 24592 | tf_op jit(solution)/shard_map/reduce_scatter | solution.py:181
  311.3 13.1 %all_gather.50 = bf16[96,256]{1,0:T(8,128)(2,1)S(1)} all-gather(bf16[24,256]{1,0:T(8,128)(2,1)S(1)} %convert_element_type.207), channel_id=1, replica_groups=mesh['seq'=8,'rows'=4] {'rows'}, dimensions={0}, use_global_device_ids=true | all-gather | bytes 61440 | tf_op jit(solution)/shard_map/all_gather | solution.py:197
  325.0 89.6 %reduce-scatter.21.cloned.1.call-done = f32[24,768]{1,0:T(8,128)} async-done(((f32[768,768]{1,0:T(8,128)}), f32[24,768]{1,0:T(8,128)}) %reduce-scatter.21.cloned.1.call-update) | async-done | bytes 73744 | tf_op jit(solution)/shard_map/reduce_scatter | solution.py:185
  415.5 13.5 %all_gather.54 = bf16[96,768]{1,0:T(8,128)(2,1)S(1)} all-gather(bf16[24,768]{1,0:T(8,128)(2,1)S(1)} %convert_element_type.215), channel_id=1, replica_groups=mesh['seq'=8,'rows'=4] {'rows'}, dimensions={0}, use_global_device_ids=true | all-gather | bytes 184320 | tf_op jit(solution)/shard_map/all_gather | solution.py:205
  429.8 88.1 %reduce-scatter.23.cloned.1.call-done = f32[24,768]{1,0:T(8,128)} async-done(((f32[768,768]{1,0:T(8,128)}), f32[24,768]{1,0:T(8,128)}) %reduce-scatter.23.cloned.1.call-update) | async-done | bytes 73744 | tf_op jit(solution)/shard_map/reduce_scatter | solution.py:186
  518.7 13.5 %all_gather.55 = bf16[96,768]{1,0:T(8,128)(2,1)S(1)} all-gather(bf16[24,768]{1,0:T(8,128)(2,1)S(1)} %convert_element_type.217), channel_id=1, replica_groups=mesh['seq'=8,'rows'=4] {'rows'}, dimensions={0}, use_global_device_ids=true | all-gather | bytes 184320 | tf_op jit(solution)/shard_map/all_gather | solution.py:206
  533.0 89.0 %reduce-scatter.19.cloned.1.call-done = f32[24,768]{1,0:T(8,128)} async-done(((f32[768,768]{1,0:T(8,128)}), f32[24,768]{1,0:T(8,128)}) %reduce-scatter.19.cloned.1.call-update) | async-done | bytes 73744 | tf_op jit(solution)/shard_map/reduce_scatter | solution.py:184
  622.9 13.8 %all_gather.53 = bf16[96,768]{1,0:T(8,128)(2,1)S(1)} all-gather(bf16[24,768]{1,0:T(8,128)(2,1)S(1)} %convert_element_type.213), channel_id=1, replica_groups=mesh['seq'=8,'rows'=4] {'rows'}, dimensions={0}, use_global_device_ids=true | all-gather | bytes 184320 | tf_op jit(solution)/shard_map/all_gather | solution.py:204
  640.9 39.3 %all-reduce.16 = (bf16[768]{0:T(1024)(128)(2,1)S(1)}, bf16[768]{0:T(1024)(128)(2,1)S(1)}, bf16[1280]{0:T(1024)(128)(2,1)S(1)}, bf16[1280]{0:T(1024)(128)(2,1)S(1...) all-reduce(f32[768]{0:T(1024)S(1)} %get-tuple-element.19, ...), channel_id=10, replica_groups=mesh['seq'=8,'rows'=4] {'seq','rows'}, use_global_device_ids=true, to_apply=%region_24.25.clone | all-reduce | flops 7168 | bytes 43008
  682.5 10.2 %all-reduce.17 = (bf16[96]{0:T(256)(128)(2,1)S(1)}, bf16[96]{0:T(256)(128)(2,1)S(1)}, bf16[160]{0:T(256)(128)(2,1)S(1)}, bf16[160]{0:T(256)(128)(2,1)S(1)}, bf16...) all-reduce(bf16[96]{0:T(256)(128)(2,1)S(1)} %dynamic-update-slice, ...), channel_id=1, replica_groups=mesh['seq'=8,'rows'=4] {'rows'}, use_global_device_ids=true, to_apply=%add | all-reduce | flops 896 | bytes 3584
  699.4 60.2 %reduce-scatter.15.cloned.1.call-done = f32[40,256]{1,0:T(8,128)} async-done(((f32[1280,256]{1,0:T(8,128)}), f32[40,256]{1,0:T(8,128)}) %reduce-scatter.15.cloned.1.call-update) | async-done | bytes 40976 | tf_op jit(solution)/shard_map/reduce_scatter | solution.py:182
  760.4 13.2 %all_gather.51 = bf16[160,256]{1,0:T(8,128)(2,1)S(1)} all-gather(bf16[40,256]{1,0:T(8,128)(2,1)S(1)} %convert_element_type.209), channel_id=1, replica_groups=mesh['seq'=8,'rows'=4] {'rows'}, dimensions={0}, use_global_device_ids=true | all-gather | bytes 102400 | tf_op jit(solution)/shard_map/all_gather | solution.py:200
  774.3 92.5 %reduce-scatter.17.cloned.1.call-done = f32[40,768]{1,0:T(8,128)} async-done(((f32[1280,768]{1,0:T(8,128)}), f32[40,768]{1,0:T(8,128)}) %reduce-scatter.17.cloned.1.call-update) | async-done | bytes 122896 | tf_op jit(solution)/shard_map/reduce_scatter | solution.py:183
  867.7 14.2 %all_gather.52 = bf16[160,768]{1,0:T(8,128)(2,1)S(1)} all-gather(bf16[40,768]{1,0:T(8,128)(2,1)S(1)} %convert_element_type.211), channel_id=1, replica_groups=mesh['seq'=8,'rows'=4] {'rows'}, dimensions={0}, use_global_device_ids=true | all-gather | bytes 307200 | tf_op jit(solution)/shard_map/all_gather | solution.py:201
  (193 shorter events, 116.1 us)
Async XLA Ops:
  7.3 37.0 %all-gather.2.cloned.1.call-start = ((), (), s32[]{:S(2)}) async-start(), calls=%async_computation.8 | async-start | bytes 2654208 | tf_op jit(solution)/shard_map/all_gather | solution.py:87
  12.4 19.6 %copy-start.20 = (s32[6,256]{1,0:T(8,128)S(1)}, s32[6,256]{1,0:T(8,128)}, u32[]{:S(2)}) copy-start(s32[6,256]{1,0:T(8,128)} %param.22) | copy-start | bytes 18436
  12.4 19.6 %copy-start.21 = (s32[6,256]{1,0:T(8,128)S(1)}, s32[6,256]{1,0:T(8,128)}, u32[]{:S(2)}) copy-start(s32[6,256]{1,0:T(8,128)} %param.21) | copy-start | bytes 18436
  12.4 19.9 %copy-start.24 = (f32[768]{0:T(1024)S(1)}, f32[768]{0:T(1024)}, u32[]{:S(2)}) copy-start(f32[768]{0:T(1024)} %param.29) | copy-start | bytes 9220
  12.4 19.9 %copy-start.30 = (f32[768]{0:T(1024)S(1)}, f32[768]{0:T(1024)}, u32[]{:S(2)}) copy-start(f32[768]{0:T(1024)} %param.30) | copy-start | bytes 9220
  12.4 157.1 %reduce-scatter.9.cloned.1.call-start = ((), (), s32[]{:S(2)}) async-start(), calls=%async_computation.9 | async-start | bytes 884736 | tf_op jit(solution)/shard_map/reduce_scatter | solution.py:150
  49.0 8.6 copy-start.4
  49.0 8.6 copy-start.26
  59.9 24.8 %copy-start.8 = (f32[6,256,768]{2,1,0:T(8,128)}, f32[6,256,768]{2,1,0:T(8,128)S(1)}, u32[]{:S(2)}) copy-start(f32[6,256,768]{2,1,0:T(8,128)S(1)} %get-tuple-element.54) | copy-start | bytes 14155780
  65.8 11.7 %copy-start.9 = (bf16[6,256,768]{2,1,0:T(8,128)(2,1)S(1)}, bf16[6,256,768]{2,1,0:T(8,128)(2,1)}, u32[]{:S(2)}) copy-start(bf16[6,256,768]{2,1,0:T(8,128)(2,1)} %param.37) | copy-start | bytes 7077892
  65.8 11.6 %copy-start.27 = (bf16[768,768]{1,0:T(8,128)(2,1)S(1)}, bf16[768,768]{1,0:T(8,128)(2,1)}, u32[]{:S(2)}) copy-start(bf16[768,768]{1,0:T(8,128)(2,1)} %param.28) | copy-start | bytes 3538948
  110.5 12.6 %copy-start.14 = (bf16[6,256,256]{1,2,0:T(8,128)(2,1)S(1)}, bf16[6,256,256]{1,2,0:T(8,128)(2,1)}, u32[]{:S(2)}) copy-start(bf16[6,256,256]{1,2,0:T(8,128)(2,1)} %copy-done.13) | copy-start | bytes 2359300
  128.2 81.0 %reduce-scatter.11.cloned.1.call-start = ((), (), s32[]{:S(2)}) async-start(), calls=%async_computation.10 | async-start | bytes 2654208 | tf_op jit(solution)/shard_map/reduce_scatter | solution.py:153
  142.0 168.5 %reduce-scatter.13.cloned.1.call-start = ((), (), s32[]{:S(2)}) async-start(), calls=%async_computation.11 | async-start | bytes 811008 | tf_op jit(solution)/shard_map/reduce_scatter | solution.py:181
  149.6 265.0 %reduce-scatter.21.cloned.1.call-start = ((), (), s32[]{:S(2)}) async-start(), calls=%async_computation.15 | async-start | bytes 2433024 | tf_op jit(solution)/shard_map/reduce_scatter | solution.py:185
  156.7 361.1 %reduce-scatter.23.cloned.1.call-start = ((), (), s32[]{:S(2)}) async-start(), calls=%async_computation.16 | async-start | bytes 2433024 | tf_op jit(solution)/shard_map/reduce_scatter | solution.py:186
  162.7 459.3 %reduce-scatter.19.cloned.1.call-start = ((), (), s32[]{:S(2)}) async-start(), calls=%async_computation.14 | async-start | bytes 2433024 | tf_op jit(solution)/shard_map/reduce_scatter | solution.py:184
  169.3 590.3 %reduce-scatter.15.cloned.1.call-start = ((), (), s32[]{:S(2)}) async-start(), calls=%async_computation.12 | async-start | bytes 1351680 | tf_op jit(solution)/shard_map/reduce_scatter | solution.py:182
  172.0 40.9 %copy-start.34 = (u32[32]{0:T(128)S(1)}, u32[32]{0:T(128)}, u32[]{:S(2)}) copy-start(u32[32]{0:T(128)} %constant.97) | copy-start | bytes 388
  172.0 694.8 %reduce-scatter.17.cloned.1.call-start = ((), (), s32[]{:S(2)}) async-start(), calls=%async_computation.13 | async-start | bytes 4055040 | tf_op jit(solution)/shard_map/reduce_scatter | solution.py:183
  212.9 7.0 slice-start
  214.9 8.2 slice-start.2
  223.1 414.4 %copy-start.17 = (bf16[6,32,768]{2,1,0:T(8,128)(2,1)S(1)}, bf16[6,32,768]{2,1,0:T(8,128)(2,1)}, u32[]{:S(2)}) copy-start(bf16[6,32,768]{2,1,0:T(8,128)(2,1)} %reduce-scatter.11.cloned.1.call-done) | copy-start | bytes 884740
  226.5 411.7 %copy-start.18 = (bf16[6,32,256]{2,1,0:T(8,128)(2,1)S(1)}, bf16[6,32,256]{2,1,0:T(8,128)(2,1)}, u32[]{:S(2)}) copy-start(bf16[6,32,256]{2,1,0:T(8,128)(2,1)} %reduce-scatter.9.cloned.1.call-done) | copy-start | bytes 294916
  (25 other events, 87.2 us)
Sparse Core Ops, SparseCore 0:
  12.5 31.6 all-gather.1
  128.4 35.0 reduce-scatter.8
  166.8 42.4 reduce-scatter.10
  215.0 95.4 reduce-scatter.12
  316.5 98.0 reduce-scatter.20
  419.8 98.0 reduce-scatter.22
  524.0 97.9 reduce-scatter.18
  624.2 135.3 reduce-scatter.14
  765.9 100.8 reduce-scatter.16
where the time goes:
time: 898 us; the launch traced here: 889 us
  waiting for transfers between devices  543 us (60%)
  blocking collectives  144 us (16%)
  matrix products  103 us (11%)
  other arithmetic  54 us (6%)
  local copies, waits for them, and re-layouts  29 us (3%)
  between operations  16.1 us (2%)
    reduce_scatter x1, waiting for transfers between devices, body(): lax.psum_scatter(grad_value_weight, ('seq', 'rows'), scatter_dimension=0,...  92.5 us
    reduce_scatter x1, waiting for transfers between devices, body(): lax.psum_scatter(grad_up_weight, ('seq', 'rows'), scatter_dimension=0, ti...  89.6 us
    reduce_scatter x1, waiting for transfers between devices, body(): lax.psum_scatter(grad_out_weight, ('seq', 'rows'), scatter_dimension=0, t...  89 us
    reduce_scatter x1, waiting for transfers between devices, body(): lax.psum_scatter(grad_down_weight, ('seq', 'rows'), scatter_dimension=0,...  88.1 us
    reduce_scatter x1, waiting for transfers between devices, body(): lax.psum_scatter(grad_query_weight, ('seq', 'rows'), scatter_dimension=0,...  84 us
    reduce_scatter x1, waiting for transfers between devices, body(): lax.psum_scatter(grad_key_weight, ('seq', 'rows'), scatter_dimension=0, t...  60.2 us
    unnamed x2, blocking collectives  49.5 us
    reduce_scatter x1, waiting for transfers between devices, body(): lax.psum_scatter(value_part.astype(jnp.bfloat16), 'seq', scatter_dimensio...  37.2 us
  transfers between devices with their start and end apart: 9, of which 8 were waited for; matrix products, arithmetic and copies ran while one was open for 10% of the time, Pallas kernels for 0%

commit v1 on v0

v1 whole, which is shorter than its diff:
```python
import functools
import types
from typing import Any, NamedTuple

import jax
import jax.numpy as jnp
from jax import lax
from jax.experimental import pallas as pl
from jax.experimental.pallas import tpu as pltpu
from jax.sharding import PartitionSpec as P

HEADS = 8
HDIM = 96
QKDIM = 32
EPS = 1e-05
SCALE = QKDIM ** (-0.5)
MESH = pl.DeviceIdType.MESH
f32, bf16 = jnp.float32, jnp.bfloat16


def dg(a, b, ca, cb):
    return lax.dot_general(a, b, (((ca,), (cb,)), ((), ())), preferred_element_type=f32)


def norm(x):
    mean = jnp.mean(x, -1, keepdims=True)
    cen = x - mean
    inv = lax.rsqrt(jnp.mean(cen * cen, -1, keepdims=True) + EPS)
    return cen * inv, inv


def norm_back(grad, gain, hat, inv):
    g = grad * gain
    return inv * (
        g - jnp.mean(g, -1, keepdims=True) - hat * jnp.mean(g * hat, -1, keepdims=True)
    )


def row_sum(x):
    n, w = x.shape
    return jnp.sum(x.reshape(n // 8, 8, w), axis=0)


def flat(x):
    return x.reshape(-1, x.shape[-1])


def add(a, b):
    return (a.astype(f32) + b.astype(f32)).astype(bf16)


class Place:
    def __init__(self, n_rows):
        self.n = n_rows
        self.s = lax.axis_index("seq")
        self.r = lax.axis_index("rows")
        self.core = lax.rem(self.s, 2)
        self.chip = self.s // 2
        self.xc = self.chip + 1 - 2 * lax.rem(self.chip, 2)
        self.yc = lax.rem(self.chip + 2, 4)
        self.dc = lax.rem(self.xc + 2, 4)
        self.sib = (self.s + 1 - 2 * self.core, self.r)
        self.xn = (2 * self.xc + self.core, self.r)
        self.yn = (2 * self.yc + self.core, self.r)
        half = n_rows // 2
        self.left = self.r < half
        self.mid = (self.r == half - 1) | (self.r == half)
        self.not_end = (self.r != 0) & (self.r != n_rows - 1)
        step = jnp.where(self.left, 1, -1)
        self.inner = (self.s, lax.rem(self.r + step + n_rows, n_rows))
        self.outer = (self.s, lax.rem(self.r - step + n_rows, n_rows))

    def barrier(self):
        bar = pltpu.get_barrier_semaphore()
        up = (self.s, lax.rem(self.r + 1, self.n))
        down = (self.s, lax.rem(self.r + self.n - 1, self.n))
        peers = [self.sib, self.xn, self.yn, up, down]
        for peer in peers:
            pl.semaphore_signal(bar, inc=1, device_id=peer, device_id_type=MESH)
        pl.semaphore_wait(bar, len(peers))


def rcopy(src, dst, ssem, rsem, peer):
    return pltpu.make_async_remote_copy(
        src_ref=src, dst_ref=dst, send_sem=ssem, recv_sem=rsem, device_id=peer, device_id_type=MESH
    )


class Line:
    def __init__(self, pc, src, zo, zi, ssem, rsem, kind):
        zt = zo
        self.pc, self.src, self.zo, self.zi, self.zt, self.kind = pc, src, zo, zi, zt, kind
        self.up_c = rcopy(src, zo, ssem.at[0], rsem.at[0], pc.inner)
        self.cross_c = rcopy(src, zi, ssem.at[1], rsem.at[1], pc.inner)
        self.down_mid = rcopy(zt, zi, ssem.at[2], rsem.at[1], pc.outer)
        self.down_far = rcopy(zi, zi, ssem.at[2], rsem.at[1], pc.outer)

    def plus(self, a, b):
        return (a.astype(f32) + b.astype(f32)).astype(self.kind)

    def up(self):
        pc = self.pc

        @pl.when(pc.not_end)
        def _():
            self.up_c.wait_recv()
            self.src[...] = self.plus(self.src[...], self.zo[...])

        pl.when(pc.mid)(self.cross_c.start)
        pl.when(jnp.logical_not(pc.mid))(self.up_c.start)

    def middle(self):
        pc = self.pc

        @pl.when(pc.mid)
        def _():
            self.cross_c.wait_recv()
            self.zt[...] = self.plus(self.src[...], self.zi[...])

        pl.when(pc.mid & pc.not_end)(self.down_mid.start)

    def down(self):
        pc = self.pc
        pl.when(jnp.logical_not(pc.mid))(self.cross_c.wait_recv)
        pl.when(jnp.logical_not(pc.mid) & pc.not_end)(self.down_far.start)

    def result(self, write):
        pc = self.pc
        pl.when(pc.mid)(lambda: write(self.zt))
        pl.when(jnp.logical_not(pc.mid))(lambda: write(self.zi))

    def drain(self):
        pc = self.pc
        pl.when(pc.mid)(self.cross_c.wait_send)
        pl.when(jnp.logical_not(pc.mid))(self.up_c.wait_send)
        pl.when(pc.mid & pc.not_end)(self.down_mid.wait_send)
        pl.when(jnp.logical_not(pc.mid) & pc.not_end)(self.down_far.wait_send)


class Scatter:
    def __init__(self, pc, part, width, l0, la, lb, la2, lb2, ssem, rsem):
        self.pc, self.part, self.l0 = pc, part, l0
        self.la, self.lb, self.la2, self.lb2 = la, lb, la2, lb2
        h = width // 2
        self.A, self.B = pl.ds(0, h), pl.ds(h, h)
        lead = (slice(None),) * (len(l0.shape) - 2)
        self.lead = lead

        def blk(chip, cols):
            return l0.at[(chip, *lead, cols)]

        self.blk = blk
        other = 1 - pc.core
        self.pair = [
            rcopy(part(2 * q + other), l0.at[q], ssem.at[q], rsem.at[q], pc.sib) for q in range(4)
        ]
        A, B = self.A, self.B
        self.first = [
            rcopy(blk(pc.xc, A), la.at[0], ssem.at[4], rsem.at[4], pc.xn),
            rcopy(blk(pc.dc, A), la.at[1], ssem.at[5], rsem.at[5], pc.xn),
            rcopy(blk(pc.yc, B), lb.at[0], ssem.at[6], rsem.at[6], pc.yn),
            rcopy(blk(pc.dc, B), lb.at[1], ssem.at[7], rsem.at[7], pc.yn),
        ]
        self.second = [
            rcopy(blk(pc.yc, A), la2, ssem.at[8], rsem.at[8], pc.yn),
            rcopy(blk(pc.xc, B), lb2, ssem.at[9], rsem.at[9], pc.xn),
        ]

    def p0(self):
        for c in self.pair:
            c.start()

    def p1(self):
        pc = self.pc
        for q in range(4):
            self.pair[q].wait_recv()
            self.l0[q] = add(self.l0[q], self.part(2 * q + pc.core)[...])
        for c in self.first:
            c.start()

    def p2(self):
        pc = self.pc
        for c in self.first:
            c.wait_recv()

        def into(chip, cols, got):
            v = self.blk(chip, cols)
            v[...] = add(v[...], got[...])

        into(pc.yc, self.A, self.la.at[1])
        into(pc.xc, self.B, self.lb.at[1])
        for c in self.second:
            c.start()
        into(pc.chip, self.A, self.la.at[0])
        into(pc.chip, self.B, self.lb.at[0])

    def p3(self):
        pc = self.pc
        for c, cols, got in zip(self.second, (self.A, self.B), (self.la2, self.lb2)):
            c.wait_recv()
            v = self.blk(pc.chip, cols)
            v[...] = add(v[...], got[...])

    def drain(self):
        for c in self.pair + self.first + self.second:
            c.wait_send()


def scatter_scratch(lead, width):
    half = width // 2
    return dict(
        l0=pltpu.VMEM((4, *lead, width), bf16),
        la=pltpu.VMEM((2, *lead, half), bf16),
        lb=pltpu.VMEM((2, *lead, half), bf16),
        la2=pltpu.VMEM((*lead, half), bf16),
        lb2=pltpu.VMEM((*lead, half), bf16),
        ssem=pltpu.SemaphoreType.DMA((10,)),
        rsem=pltpu.SemaphoreType.DMA((10,)),
    )


def line_scratch(shape, kind):
    return dict(
        zo=pltpu.VMEM(shape, kind),
        zi=pltpu.VMEM(shape, kind),
        ssem=pltpu.SemaphoreType.DMA((3,)),
        rsem=pltpu.SemaphoreType.DMA((2,)),
    )


class Gather:
    def __init__(self, pc, kv, rows, ssem, rsem):
        def blk(t, cols=slice(None)):
            return kv.at[rows, pl.ds(pl.multiple_of(t * 32, 32), 32), cols]

        h = kv.shape[-1] // 2
        A, B = pl.ds(0, h), pl.ds(h, h)
        ds_ = 2 * pc.dc + pc.core

        def copy(k, ref, peer):
            return rcopy(ref, ref, ssem.at[k], rsem.at[k], peer)

        self.own = [copy(0, blk(pc.s), pc.sib), copy(1, blk(pc.s), pc.xn), copy(2, blk(pc.s), pc.yn)]
        self.from_x = [copy(3, blk(pc.xn[0], A), pc.yn), copy(4, blk(pc.xn[0]), pc.sib)]
        self.from_y = [copy(5, blk(pc.yn[0], B), pc.xn), copy(6, blk(pc.yn[0]), pc.sib)]
        self.from_d = [copy(7, blk(ds_, A), pc.sib), copy(8, blk(ds_, B), pc.sib)]

    def p0(self):
        for c in self.own[::-1]:
            c.start()

    def p1(self):
        self.own[1].wait_recv()
        for c in self.from_x:
            c.start()
        self.own[2].wait_recv()
        for c in self.from_y:
            c.start()

    def p2(self):
        self.from_x[0].wait_recv()
        self.from_d[0].start()
        self.from_y[0].wait_recv()
        self.from_d[1].start()

    def p3(self):
        for c in (self.own[0], self.from_x[1], self.from_y[1], *self.from_d):
            c.wait_recv()

    def drain(self):
        for c in self.own + self.from_x + self.from_y + self.from_d:
            c.wait_send()


def kernel(n_rows, names, *refs):
    R = types.SimpleNamespace(**dict(zip(names, refs, strict=True)))
    q_hbm, c_hbm, lat_hbm = R.queries, R.cotangent, R.latents
    line_of = lambda ref: ref[...].reshape(1, -1)
    q_ref, c_ref, lat_ref = R.q_v, R.c_v, R.lat_v
    wq, wk, wv, wo, wu, wd = R.wq_v, R.wk_v, R.wv_v, R.wo_v, R.wu_v, R.wd_v
    kv, qn_s, qp_s, p_s, mix_s, hn_s = R.kv, R.qn, R.qp, R.p, R.mix, R.hn
    act_s, dpre_s, dres_s, dm_s, dq_s = R.act, R.dpre, R.dres, R.dm, R.dq
    bo_v, gq_v, s_scr = R.bo_v, R.gq_v, R.s_scr
    lidT, ln_s, dkv_own, vec = R.lidT, R.ln, R.dkv_own, R.vec
    rows, positions, width = q_ref.shape
    lats, lwidth = lat_ref.shape[1:]
    pair = 2
    n_pairs = rows // pair
    tokens = rows * positions
    span = positions * pair

    loads = {}
    for k, (name, src, dst) in enumerate(
        [
            ("lat", lat_hbm, lat_ref),
            ("wk", R.key_weight, wk),
            ("wv", R.value_weight, wv),
            ("q", q_hbm, q_ref),
            ("wq", R.query_weight, wq),
            ("wo", R.out_weight, wo),
            ("wu", R.up_weight, wu),
            ("wd", R.down_weight, wd),
            ("c", c_hbm, c_ref),
        ]
    ):
        loads[name] = pltpu.make_async_copy(src, dst, R.load_sem.at[k])
        loads[name].start()

    pc = Place(n_rows)
    pc.barrier()

    def loop(first, last, body):
        def step(i, carry):
            body(i)
            return carry

        lax.fori_loop(first, last, step, 0)

    lane1 = lax.broadcasted_iota(jnp.int32, (1, 128), 1)

    def head_mask(hh, kind):
        return ((lane1 >= QKDIM * hh) & (lane1 < QKDIM * (hh + 1))).astype(kind)

    own = pl.ds(pl.multiple_of(pc.s * lats, lats), lats)

    def l0(g):
        rs = pl.ds(g * pair, pair)
        hat, _ = norm(flat(lat_ref[rs]).astype(f32))
        ln = (hat * line_of(R.gain_latent) + line_of(R.shift_latent)).astype(bf16)
        ln_s[pl.ds(g * pair * lats, pair * lats), :] = ln
        k = dg(ln, wk[...], 1, 0).astype(bf16)
        v = dg(ln, wv[...], 1, 0).astype(bf16)
        kv[rs, own, 0:256] = k.reshape(pair, lats, -1)
        kv[rs, own, 256:1024] = v.reshape(pair, lats, -1)

    def at(i):
        return pl.ds(pl.multiple_of(i * span, span), span)

    def row(r):
        return pl.ds(pl.multiple_of(r * positions, positions), positions)

    def f1(i):
        hat, _ = norm(flat(q_ref[pl.ds(i * pair, pair)]).astype(f32))
        qn = (hat * line_of(R.gain_query) + line_of(R.shift_query)).astype(bf16)
        qn_s[at(i), :] = qn
        qp_s[at(i), :] = (dg(qn, wq[...], 1, 0) * SCALE).astype(bf16)

    def f1b(i):
        c = flat(c_ref[pl.ds(i * pair, pair)])
        vec[5, :, :width] += row_sum(c.astype(f32))
        dpre_s[at(i), :] = dg(c, wd[...], 1, 1).astype(bf16)

    def spot(r, h):
        return pl.ds(pl.multiple_of((r * HEADS + h) * 256, 256), 256)

    def spots(r, g):
        return pl.ds(pl.multiple_of((r * HEADS + 4 * g) * 256, 1024), 1024)

    def f2(r):
        k = kv[r, :, :256]
        vT = kv[r, :, 256:].T
        lane = lax.broadcasted_iota(jnp.int32, (256, 128), 1)
        col = jnp.sum(jnp.where(lane == r, lidT[...], 0.0), axis=1, keepdims=True)
        allowed = col == R.query_ids[pl.ds(r, 1), :].astype(f32)
        for g in range(2):
            kb = k[:, 128 * g : 128 * g + 128]
            km = jnp.concatenate([kb * head_mask(hh, bf16) for hh in range(4)], axis=0)
            sg = dg(km, qp_s[row(r), 128 * g : 128 * g + 128], 1, 1)
            for hh in range(4):
                s_scr[4 * g + hh] = sg[256 * hh : 256 * (hh + 1)]
        for h in range(HEADS):
            s = jnp.where(allowed, s_scr[h], -1e30)
            e = jnp.exp(s - jnp.max(s, axis=0, keepdims=True))
            p_s[spot(r, h), :] = (e * (1.0 / jnp.sum(e, axis=0, keepdims=True))).astype(bf16)
        for h in range(HEADS):
            hs = slice(HDIM * h, HDIM * (h + 1))
            mix_s[hs, row(r)] = dg(vT[hs], p_s[spot(r, h), :], 1, 0).astype(bf16)


    def put_out(i):
        return pltpu.make_async_copy(bo_v, R.block_out.at[pl.ds(i * pair, pair)], R.bo_sem)

    def put_gq(r):
        return pltpu.make_async_copy(gq_v, R.grad_queries.at[r], R.gq_sem)

    def f3(i):
        rs = pl.ds(i * pair, pair)
        resid = flat(q_ref[rs]).astype(f32) + dg(mix_s[:, at(i)], wo[...], 0, 0)
        hat, inv = norm(resid)
        hn = (hat * line_of(R.gain_hidden) + line_of(R.shift_hidden)).astype(bf16)
        hn_s[at(i), :] = hn
        pre = dg(hn, wu[...], 1, 0) + line_of(R.bias_up)
        phi = 0.5 * (1.0 + lax.erf(pre * (0.5**0.5)))
        act = (pre * phi).astype(bf16)
        act_s[at(i), :] = act
        slope = phi + pre * (jnp.exp(-0.5 * pre * pre) * 0.3989422804014327)
        dpre = (dpre_s[at(i), :].astype(f32) * slope).astype(bf16)
        dpre_s[at(i), :] = dpre

        @pl.when(i >= 1)
        def _():
            put_out(i - 1).wait()

        out = (resid + dg(act, wd[...], 1, 0) + line_of(R.bias_down)).astype(bf16)
        bo_v[...] = out.reshape(bo_v.shape)
        put_out(i).start()
        vec[4, :, :width] += row_sum(dpre.astype(f32))
        dh = dg(dpre, wu[...], 1, 1)
        vec[2, :, :width] += row_sum(dh * hat)
        vec[3, :, :width] += row_sum(dh)
        cf = flat(c_ref[rs]).astype(f32)
        dlow = (norm_back(dh, line_of(R.gain_hidden), hat, inv) + cf).astype(bf16)
        dres_s[at(i), :] = dlow
        dm_s[:, at(i)] = dg(wo[...], dlow, 1, 1).astype(bf16)

    def b2(r):
        k = kv[r, :, :256]
        kT = k.T
        v = kv[r, :, 256:]
        dvs, dqs, dks = [], [], []
        for h in range(HEADS):
            hs = slice(HDIM * h, HDIM * (h + 1))
            s_scr[h] = dg(v[:, hs], dm_s[hs, row(r)], 1, 0)
        for h in range(HEADS):
            hs = slice(HDIM * h, HDIM * (h + 1))
            dvs.append(dg(dm_s[hs, row(r)], p_s[spot(r, h), :], 1, 1).astype(bf16))
        for h in range(HEADS):
            p = p_s[spot(r, h), :].astype(f32)
            pd = p * s_scr[h]
            ds = pd - p * jnp.sum(pd, axis=0, keepdims=True)
            p_s[spot(r, h), :] = ds.astype(bf16)
        for g in range(2):
            t = dg(p_s[spots(r, g), :], qp_s[row(r), 128 * g : 128 * g + 128], 1, 0)
            dks.append(sum(t[256 * hh : 256 * (hh + 1)] * head_mask(hh, f32) for hh in range(4)))
        for h in range(HEADS):
            kh = kT[QKDIM * h : QKDIM * (h + 1)]
            dqs.append(dg(kh, p_s[spot(r, h), :], 1, 0).astype(bf16))
        dq_s[row(r), :] = jnp.concatenate(dqs, axis=0).T
        kv[r, :, :128] = dks[0].astype(bf16)
        kv[r, :, 128:256] = dks[1].astype(bf16)
        kv[r, :, 256:] = jnp.concatenate(dvs, axis=0).T

    def b3(r):
        dqn = dg(dq_s[row(r), :], wq[...], 1, 1) * SCALE
        hat, inv = norm(q_ref[r].astype(f32))
        vec[0, :, :width] += row_sum(dqn * hat)
        vec[1, :, :width] += row_sum(dqn)

        got = norm_back(dqn, line_of(R.gain_query), hat, inv) + dres_s[row(r), :].astype(f32)

        @pl.when(r >= 1)
        def _():
            put_gq(r - 1).wait()

        gq_v[...] = got
        put_gq(r).start()

    def cols(j):
        return pl.ds(pl.multiple_of(j * 256, 256), 256)

    g_up, g_out = act_s.at[pl.ds(0, width)], hn_s.at[pl.ds(0, width)]

    def w_down():
        R.g_down[...] = dg(act_s[...], flat(c_ref[...]), 0, 0).astype(bf16)

    def w_up():
        g_up[...] = dg(hn_s[...], dpre_s[...], 0, 0).astype(bf16)

    def w_out():
        g_out[...] = dg(mix_s[...], dres_s[...], 1, 0).astype(bf16)

    def w_q():
        R.g_q[...] = (dg(qn_s[...], dq_s[...], 0, 0) * SCALE).astype(bf16)

    def w_kv(j):
        got = dg(ln_s[:, cols(j)], dkv_own[...], 0, 0).astype(bf16)
        for k in range(4):
            to = pl.ds(pl.multiple_of(k * lwidth + j * 256, 256), 256)
            p_s[to, :] = got[:, 256 * k : 256 * (k + 1)]

    put_gl = [
        pltpu.make_async_copy(
            s_scr.at[k, pl.ds(0, rows * lats)], R.grad_latents.at[:, pl.ds(256 * k, 256)], R.gl_sem.at[k]
        )
        for k in range(lwidth // 256)
    ]

    def l1():
        d = dg(dkv_own[:, :256], wk[...], 1, 1) + dg(dkv_own[:, 256:], wv[...], 1, 1)
        hat, inv = norm(flat(lat_ref[...]).astype(f32))
        vec[6] += row_sum(d * hat)
        vec[7] += row_sum(d)
        got = norm_back(d, line_of(R.gain_latent), hat, inv)
        for k, c in enumerate(put_gl):
            s_scr[k, : rows * lats, :] = got[:, 256 * k : 256 * (k + 1)]
            c.start()

    gathers = [
        Gather(pc, kv, pl.ds(g * pair, pair), R.ag_s.at[g], R.ag_r.at[g]) for g in range(n_pairs)
    ]
    scat, line = {}, {}
    for name, ref, lo, n in (
        ("down", R.g_down, 0, width),
        ("up", act_s, 0, width),
        ("out", hn_s, 0, width),
        ("q", R.g_q, 0, 256),
        *((f"kv{k}", p_s, k * lwidth, 256) for k in range(4)),
    ):
        block = (lwidth if ref is p_s else width) // 8

        def part(t, ref=ref, lo=lo, block=block):
            return ref.at[pl.ds(pl.multiple_of(lo + t * block, 32), block), :]

        sc = R.sc[name]
        scat[name] = Scatter(pc, part, n, **sc)
        line[name] = Line(pc, sc["l0"].at[pc.chip], kind=bf16, **R.li[name])
    for g in range(n_pairs):

        def part(t, g=g):
            return kv.at[pl.ds(g * pair, pair), pl.ds(pl.multiple_of(t * lats, lats), lats), :]

        scat[f"d{g}"] = Scatter(pc, part, 1024, **R.sc[f"d{g}"])

    def keep(g):
        dkv_own[pl.ds(g * pair * lats, pair * lats), :] = flat(R.sc[f"d{g}"]["l0"][pc.chip])

    vec[...] = jnp.zeros_like(vec)
    lid = R.latent_ids[...].astype(f32)
    lidT[...] = jnp.concatenate([lid, jnp.zeros((128 - rows, lid.shape[1]), f32)], axis=0).T
    G0, G1, G2 = gathers
    d0, d1, d2 = (scat[f"d{g}"] for g in range(3))
    D, U, O, Q = (scat[k] for k in ("down", "up", "out", "q"))
    LD, LU, LO, LQ = (line[k] for k in ("down", "up", "out", "q"))
    for k in ("lat", "wk", "wv"):
        loads[k].wait()
    l0(0)
    G0.p0()
    l0(1)
    l0(2)
    for k in ("q", "wq"):
        loads[k].wait()
    loop(0, n_pairs, f1)
    G0.p1()
    G1.p0()
    for k in ("c", "wd"):
        loads[k].wait()
    loop(0, n_pairs, f1b)
    G0.p2()
    G0.p3()
    for k in ("wo", "wu"):
        loads[k].wait()
    hooks = {
        0: ([G1.p1, G2.p0], [G1.p2, G1.p3, G2.p1, G0.drain], [d0.p0]),
        1: ([d0.p1, G2.p2], [d0.p2, G2.p3, G1.drain], [d0.p3, lambda: keep(0), d1.p0]),
        2: ([d1.p1], [d1.p2, G2.drain], []),
    }

    def hook(i, k):
        for p, fns in hooks.items():
            if fns[k]:

                @pl.when(i == p)
                def _():
                    for fn in fns[k]:
                        fn()

    def main(i):
        loop(i * pair, i * pair + pair, f2)
        hook(i, 0)
        f3(i)
        hook(i, 1)

        @pl.when(i < n_pairs - 1)
        def _():
            loop(i * pair, i * pair + pair, b2)

        hook(i, 2)

    loop(0, n_pairs, main)
    w_down()
    D.p0()
    d1.p3()
    keep(1)
    w_up()
    U.p0()
    D.p1()
    w_out()
    O.p0()
    U.p1()
    D.p2()
    b2(rows - 2)
    O.p1()
    b2(rows - 1)
    d2.p0()
    D.p3()
    LD.up()
    U.p2()
    loop(0, 3, b3)
    d2.p1()
    O.p2()
    U.p3()
    LU.up()
    LD.middle()
    loop(3, rows, b3)
    d2.p2()
    w_q()
    Q.p0()
    O.p3()
    LO.up()
    LU.middle()
    LD.down()
    d2.p3()
    keep(2)
    Q.p1()
    loop(0, 5, w_kv)
    KV = [scat[f"kv{k}"] for k in range(4)]
    LKV = [line[f"kv{k}"] for k in range(4)]
    for K in KV:
        K.p0()
    l1()
    vtot = R.vtot
    vtot[0] = jnp.sum(vec[...], axis=1)
    vsteps = [
        rcopy(vtot.at[k], R.vland.at[k], R.vs.at[k], R.vr.at[k], peer)
        for k, peer in enumerate((pc.sib, pc.xn, pc.yn))
    ]
    lv = Line(pc, vtot.at[3], kind=f32, **R.ln_vec)

    def vstep(k):
        vsteps[k].wait_recv()
        vtot[k + 1] = vtot[k] + R.vland[k]

    LO.middle()
    LU.down()
    vsteps[0].start()
    KV[0].p1()
    KV[1].p1()
    vstep(0)
    vsteps[1].start()
    Q.p2()
    KV[2].p1()
    LO.down()
    KV[3].p1()
    KV[0].p2()
    vstep(1)
    vsteps[2].start()
    KV[1].p2()
    Q.p3()
    LQ.up()
    KV[0].p3()
    LKV[0].up()
    KV[2].p2()
    KV[1].p3()
    LKV[1].up()
    vstep(2)
    lv.up()
    KV[3].p2()
    LQ.middle()
    LKV[0].middle()
    KV[2].p3()
    LKV[2].up()
    LKV[1].middle()
    lv.middle()
    KV[3].p3()
    LKV[3].up()
    LQ.down()
    LKV[0].down()
    LKV[2].middle()
    LKV[1].down()
    lv.down()
    LKV[3].middle()
    LKV[2].down()
    LKV[3].down()

    totals = []
    for k, (name, out) in enumerate(
        (
            ("down", R.t_down),
            ("up", R.t_up),
            ("out", R.t_out),
            ("q", R.t_q),
            *((f"kv{j}", R.t_kv.at[j]) for j in range(4)),
            ("v", R.t_vec),
        )
    ):
        sem = R.t_sem.at[k]
        x = line.get(name, lv)
        x.result(lambda src, out=out, sem=sem: pltpu.make_async_copy(src, out, sem).start())
        totals.append(pltpu.make_async_copy(x.zt, out, sem))
    for c in totals:
        c.wait()
    for x in (*scat.values(), *line.values(), lv):
        x.drain()
    for c in vsteps:
        c.wait_send()
    put_out(n_pairs - 1).wait()
    put_gq(rows - 1).wait()
    for c in put_gl:
        c.wait()


def unpack(*refs):
    block_out, grad_queries, grad_latents, t_down, t_up, t_out, t_q, t_kv, t_vec = refs[:9]
    out = Outs(*refs[9 : 9 + len(Outs._fields)])
    through = refs[9 + len(Outs._fields) :]
    rows = block_out.shape[0]
    step = rows // 3
    pipes = []
    for k, (src, dst) in enumerate(
        ((grad_queries, out.grad_queries), (block_out, out.block_out), (grad_latents, out.grad_latents))
    ):
        via, sem_in, sem_out = through[3 * k : 3 * k + 3]
        for j in range(3):
            rs = pl.ds(j * step, step)
            inward = pltpu.make_async_copy(src.at[rs], via.at[rs], sem_in.at[j])
            pipes.append((inward, pltpu.make_async_copy(via.at[rs], dst.at[rs], sem_out.at[j])))
    for inward, _ in pipes:
        inward.start()

    def spread():
        out.grad_down_weight[...] = t_down[...].astype(f32)
        out.grad_up_weight[...] = t_up[...].astype(f32)
        out.grad_out_weight[...] = t_out[...].astype(f32)
        out.grad_query_weight[...] = t_q[...].astype(f32)
        out.grad_key_weight[...] = t_kv[0].astype(f32)
        for k in range(3):
            out.grad_value_weight[:, 256 * k : 256 * (k + 1)] = t_kv[k + 1].astype(f32)
        vectors = (
            out.grad_gain_query,
            out.grad_shift_query,
            out.grad_gain_hidden,
            out.grad_shift_hidden,
            out.grad_bias_up,
            out.grad_bias_down,
            out.grad_gain_latent,
            out.grad_shift_latent,
        )
        for t in range(8):

            @pl.when(lax.axis_index("seq") == t)
            def _():
                for k, ref in enumerate(vectors):
                    n = ref.shape[0]
                    ref[...] = t_vec[k, n * t : n * (t + 1)]

    for inward, outward in pipes:
        inward.wait()
        outward.start()
    spread()
    for _, outward in pipes:
        outward.wait()


class Args(NamedTuple):
    queries: Any
    latents: Any
    query_ids: Any
    latent_ids: Any
    query_weight: Any
    key_weight: Any
    value_weight: Any
    out_weight: Any
    up_weight: Any
    down_weight: Any
    gain_query: Any
    shift_query: Any
    gain_latent: Any
    shift_latent: Any
    gain_hidden: Any
    shift_hidden: Any
    bias_up: Any
    bias_down: Any
    cotangent: Any


class Outs(NamedTuple):
    block_out: Any
    grad_queries: Any
    grad_latents: Any
    grad_query_weight: Any
    grad_key_weight: Any
    grad_value_weight: Any
    grad_out_weight: Any
    grad_up_weight: Any
    grad_down_weight: Any
    grad_gain_query: Any
    grad_shift_query: Any
    grad_gain_latent: Any
    grad_shift_latent: Any
    grad_gain_hidden: Any
    grad_shift_hidden: Any
    grad_bias_up: Any
    grad_bias_down: Any


def body(n_rows, n_seq, *args):
    A = Args(*args)
    rows, pos, width = A.queries.shape
    lats, lwidth = A.latents.shape[1:]
    nl = lats * n_seq
    F_ = lambda *s: jax.ShapeDtypeStruct(s, f32)
    wide, vec, lvec = F_(width // n_seq, width), F_(width // n_seq), F_(lwidth // n_seq)
    out = Outs(
        block_out=jax.ShapeDtypeStruct((rows, pos, width), bf16),
        grad_queries=F_(rows, pos, width),
        grad_latents=F_(rows, lats, lwidth),
        grad_query_weight=F_(width // n_seq, 256),
        grad_key_weight=F_(lwidth // n_seq, 256),
        grad_value_weight=F_(lwidth // n_seq, width),
        grad_out_weight=wide,
        grad_up_weight=wide,
        grad_down_weight=wide,
        grad_gain_query=vec,
        grad_shift_query=vec,
        grad_gain_latent=lvec,
        grad_shift_latent=lvec,
        grad_gain_hidden=vec,
        grad_shift_hidden=vec,
        grad_bias_up=vec,
        grad_bias_down=vec,
    )
    V = lambda *s: pltpu.VMEM(s, bf16)
    F = lambda *s: pltpu.VMEM(s, f32)
    dma = lambda *s: pltpu.SemaphoreType.DMA(s)
    tok = V(rows, pos, width)
    tok2 = V(rows * pos, width)
    tokT = V(width, rows * pos)
    scratch = dict(
        q_v=tok,
        c_v=tok,
        lat_v=V(rows, lats, lwidth),
        wq_v=V(width, 256),
        wk_v=V(lwidth, 256),
        wv_v=V(lwidth, width),
        wo_v=V(width, width),
        wu_v=V(width, width),
        wd_v=V(width, width),
        kv=V(rows, nl, 1024),
        qn=tok2,
        qp=V(rows * pos, 256),
        s_scr=F(HEADS, nl, pos),
        p=V(rows * HEADS * nl, pos),
        mix=tokT,
        hn=tok2,
        act=tok2,
        dpre=tok2,
        dres=tok2,
        dm=tokT,
        dq=V(rows * pos, 256),
        lidT=F(nl, 128),
        ln=V(rows * lats, lwidth),
        dkv_own=V(rows * lats, 1024),
        vec=F(8, 8, lwidth),
        vtot=F(4, 8, lwidth),
        vland=F(3, 8, lwidth),
        vs=dma(3),
        vr=dma(3),
        bo_v=V(2, pos, width),
        gq_v=F(pos, width),
        bo_sem=pltpu.SemaphoreType.DMA(()),
        gq_sem=pltpu.SemaphoreType.DMA(()),
        gl_sem=dma(lwidth // 256),
        t_sem=dma(9),
        load_sem=dma(9),
        ag_s=dma(rows // 2, 9),
        ag_r=dma(rows // 2, 9),
        g_down=V(width, width),
        g_q=V(width, 256),
        ln_vec=line_scratch((8, lwidth), f32),
    )
    lead, llead = (width // n_seq,), (lwidth // n_seq,)
    scratch["sc"] = dict(
        down=scatter_scratch(lead, width),
        up=scatter_scratch(lead, width),
        out=scatter_scratch(lead, width),
        q=scatter_scratch(lead, 256),
        **{f"d{g}": scatter_scratch((2, lats), 1024) for g in range(rows // 2)},
        **{f"kv{k}": scatter_scratch(llead, 256) for k in range(4)},
    )
    scratch["li"] = dict(
        down=line_scratch((*lead, width), bf16),
        up=line_scratch((*lead, width), bf16),
        out=line_scratch((*lead, width), bf16),
        q=line_scratch((*lead, 256), bf16),
        **{f"kv{k}": line_scratch((*llead, 256), bf16) for k in range(4)},
    )
    any_ = pl.BlockSpec(memory_space=pl.ANY)
    vm = pl.BlockSpec(memory_space=pltpu.VMEM)
    far = (A.queries, A.cotangent, A.latents, *A[4:10])
    in_specs = [any_ if any(a is f for f in far) else vm for a in A]
    sds = jax.ShapeDtypeStruct
    mid = dict(
        block_out=out.block_out,
        grad_queries=out.grad_queries,
        grad_latents=F_(rows * lats, lwidth),
        t_down=sds(wide.shape, bf16),
        t_up=sds(wide.shape, bf16),
        t_out=sds(wide.shape, bf16),
        t_q=sds((width // n_seq, 256), bf16),
        t_kv=sds((4, lwidth // n_seq, 256), bf16),
        t_vec=sds((8, lwidth), f32),
    )
    names = (*Args._fields, *mid, *scratch)
    flops = 2 * rows * pos * width * width * 14
    got = pl.pallas_call(
        functools.partial(kernel, n_rows, names),
        out_shape=tuple(mid.values()),
        in_specs=in_specs,
        out_specs=(any_,) * len(mid),
        scratch_shapes=list(scratch.values()),
        compiler_params=pltpu.CompilerParams(
            collective_id=0, has_side_effects=True, vmem_limit_bytes=64 << 20
        ),
        cost_estimate=pl.CostEstimate(flops=flops, bytes_accessed=24 << 20, transcendentals=0),
    )(*A)
    got = (*got[:2], got[2].reshape(rows, lats, lwidth), *got[3:])
    return pl.pallas_call(
        unpack,
        out_shape=tuple(out),
        in_specs=[any_] * 3 + [vm] * 6,
        out_specs=(any_,) * 3 + (vm,) * 14,
        scratch_shapes=[
            x
            for o in (out.grad_queries, out.block_out, out.grad_latents)
            for x in (pltpu.VMEM(o.shape, o.dtype), dma(3), dma(3))
        ],
        compiler_params=pltpu.CompilerParams(vmem_limit_bytes=64 << 20),
        cost_estimate=pl.CostEstimate(flops=0, bytes_accessed=18 << 20, transcendentals=0),
    )(*got)


def solution(mesh):
    seq = P("rows", "seq", None)
    rep = P()
    in_specs = (seq, seq, P("rows", "seq"), P("rows", None)) + (rep,) * 14 + (seq,)
    out_specs = (seq,) * 3 + (P("seq", None),) * 6 + (P("seq"),) * 8
    return jax.shard_map(
        functools.partial(body, mesh.shape["rows"], mesh.shape["seq"]),
        mesh=mesh,
        in_specs=in_specs,
        out_specs=out_specs,
        check_vma=False,
    )
```

time: 898 us -> 128 us (0.14)
  waiting for transfers between devices: 543 us -> 0 us
  blocking collectives: 144 us -> 0 us
  Pallas kernels: 0 us -> 127 us
  matrix products: 103 us -> 0 us
  other arithmetic: 54 us -> 0 us
  local copies, waits for them, and re-layouts: 29 us -> 0 us
  between operations: 16.1 us -> 0.85 us
    reduce_scatter x8 -> x0, waiting for transfers between devices: 541 us -> none  [the longest x1 92.5 us: body(): lax.psum_scatter(grad_value_weight, ('seq', 'rows'), scatter_dimension=0,...]
    pallas_call x0 -> x2, Pallas kernels: none -> 127 us  [the longest x1 118 us: body(): pl.pallas_call(functools.partial(kernel, n_rows, names), out_shape=tuple(...]
    dot_general x24 -> x0, matrix products: 103 us -> none  [the longest x6 28.1 us: weight_grad(): jnp.einsum('rqi,rqj->ij', left, right, preferred_element_type=jnp.float32)]
    all_gather x7 -> x0, blocking collectives: 94.3 us -> none  [the longest x1 14.2 us: body(): lax.all_gather(g_value.astype(jnp.bfloat16), 'rows', axis=0, tiled=True)]
    unnamed x2 -> x0, blocking collectives: 49.5 us -> none
    convert_element_type x22 -> x0, other arithmetic: 35.3 us -> none  [the longest x1 11.6 us: body(): act = act_value.astype(jnp.bfloat16)]
    reduce_sum x7 -> x0, other arithmetic: 12.8 us -> none  [the longest x3 4.45 us: normalize(): inverse = lax.rsqrt(jnp.mean(center * center, axis=-1, keepdims=True) + EPS)]
    unnamed x105 -> x0, local copies, waits for them, and re-layouts: 12 us -> none
  transfers between devices with their start and end apart: 9 -> 0, of which waited for: 8 -> 0; matrix products, arithmetic and copies ran while one was open for 10% -> 0% of each run, Pallas kernels for 0% -> 0%
where the time goes in v1:
time: 128 us
  Pallas kernels  127 us (99%)
    pallas_call x1, Pallas kernels, body(): pl.pallas_call(functools.partial(kernel, n_rows, names), out_shape=tuple(...  118 us
    pallas_call x1, Pallas kernels, body(): pl.pallas_call(unpack, out_shape=tuple(out), in_specs=[any_] * 3 + [vm] *...  8.97 us

profile of v1, /device:TPU:0, one launch (start us, length us, event | category | flops | bytes accessed | tf_op | source)
XLA Modules:
  0.0 127.7 jit_solution(9803487183618018537)
XLA Ops:
  0.7 117.9 %shard_map.314 = (bf16[6,256,768]{2,1,0:T(8,128)(2,1)}, f32[6,256,768]{2,1,0:T(8,128)}, f32[192,1280]{1,0:T(8,128)}, bf16[96,768]{1,0:T(8,128)(2,1)}, bf16[96,76...) custom-call(bf16[6,256,768]{2,1,0:T(8,128)(2,1)} %refs_0_.1, ...), custom_call_target="tpu_custom_call" | custom-call | flops 25367150592 | bytes 25165824 | tf_op jit(solution)/shard_map/pallas_call | solution.py:905
  118.6 9.0 %shard_map.315 = (bf16[6,256,768]{2,1,0:T(8,128)(2,1)}, f32[6,256,768]{2,1,0:T(8,128)}, f32[6,32,1280]{2,1,0:T(8,128)}, f32[96,256]{1,0:T(8,128)}, f32[160,256]{...) custom-call(bf16[6,256,768]{2,1,0:T(8,128)(2,1)} %get-tuple-element., ...), custom_call_target="tpu_custom_call" | custom-call | bytes 18874368 | tf_op jit(solution)/shard_map/pallas_call | solution.py:917

commit v2 on v1

v2 whole, which is shorter than its diff:
```python
import functools
import types
from typing import Any, NamedTuple

import jax
import jax.numpy as jnp
from jax import lax
from jax.experimental import pallas as pl
from jax.experimental.pallas import tpu as pltpu
from jax.sharding import PartitionSpec as P

HEADS = 8
HDIM = 96
QKDIM = 32
EPS = 1e-05
SCALE = QKDIM ** (-0.5)
MESH = pl.DeviceIdType.MESH
f32, bf16 = jnp.float32, jnp.bfloat16


def dg(a, b, ca, cb):
    return lax.dot_general(a, b, (((ca,), (cb,)), ((), ())), preferred_element_type=f32)


def norm(x):
    mean = jnp.mean(x, -1, keepdims=True)
    cen = x - mean
    inv = lax.rsqrt(jnp.mean(cen * cen, -1, keepdims=True) + EPS)
    return cen * inv, inv


def norm_back(grad, gain, hat, inv):
    g = grad * gain
    return inv * (
        g - jnp.mean(g, -1, keepdims=True) - hat * jnp.mean(g * hat, -1, keepdims=True)
    )


def row_sum(x):
    n, w = x.shape
    return jnp.sum(x.reshape(n // 8, 8, w), axis=0)


def flat(x):
    return x.reshape(-1, x.shape[-1])


def add(a, b):
    return (a.astype(f32) + b.astype(f32)).astype(bf16)


class Place:
    def __init__(self, n_rows):
        self.n = n_rows
        self.s = lax.axis_index("seq")
        self.r = lax.axis_index("rows")
        self.core = lax.rem(self.s, 2)
        self.chip = self.s // 2
        self.xc = self.chip + 1 - 2 * lax.rem(self.chip, 2)
        self.yc = lax.rem(self.chip + 2, 4)
        self.dc = lax.rem(self.xc + 2, 4)
        self.xb, self.yb = lax.rem(self.chip, 2), self.chip // 2
        self.sib = (self.s + 1 - 2 * self.core, self.r)
        self.xn = (2 * self.xc + self.core, self.r)
        self.yn = (2 * self.yc + self.core, self.r)
        half = n_rows // 2
        self.left = self.r < half
        self.mid = (self.r == half - 1) | (self.r == half)
        self.not_end = (self.r != 0) & (self.r != n_rows - 1)
        step = jnp.where(self.left, 1, -1)
        self.inner = (self.s, lax.rem(self.r + step + n_rows, n_rows))
        self.outer = (self.s, lax.rem(self.r - step + n_rows, n_rows))

    def greet(self):
        up = (self.s, lax.rem(self.r + 1, self.n))
        down = (self.s, lax.rem(self.r + self.n - 1, self.n))
        self.bar = pltpu.get_barrier_semaphore()
        for peer in (self.sib, self.xn, self.yn, up, down):
            pl.semaphore_signal(self.bar, inc=1, device_id=peer, device_id_type=MESH)

    def met(self):
        pl.semaphore_wait(self.bar, 5)


def rcopy(src, dst, ssem, rsem, peer):
    return pltpu.make_async_remote_copy(
        src_ref=src, dst_ref=dst, send_sem=ssem, recv_sem=rsem, device_id=peer, device_id_type=MESH
    )


class Line:
    def __init__(self, pc, src, zo, zi, ssem, rsem, kind):
        zt = zo
        self.pc, self.src, self.zo, self.zi, self.zt, self.kind = pc, src, zo, zi, zt, kind
        self.up_c = rcopy(src, zo, ssem.at[0], rsem.at[0], pc.inner)
        self.cross_c = rcopy(src, zi, ssem.at[1], rsem.at[1], pc.inner)
        self.down_mid = rcopy(zt, zi, ssem.at[2], rsem.at[1], pc.outer)
        self.down_far = rcopy(zi, zi, ssem.at[2], rsem.at[1], pc.outer)

    def plus(self, a, b):
        return (a.astype(f32) + b.astype(f32)).astype(self.kind)

    def send(self):
        pc = self.pc
        pl.when(jnp.logical_not(pc.not_end) & jnp.logical_not(pc.mid))(self.up_c.start)

    def up(self):
        pc = self.pc

        @pl.when(pc.not_end)
        def _():
            self.up_c.wait_recv()
            self.src[...] = self.plus(self.src[...], self.zo[...])

        pl.when(pc.mid)(self.cross_c.start)
        pl.when(jnp.logical_not(pc.mid) & pc.not_end)(self.up_c.start)

    def middle(self):
        pc = self.pc

        @pl.when(pc.mid)
        def _():
            self.cross_c.wait_recv()
            self.zt[...] = self.plus(self.src[...], self.zi[...])

        pl.when(pc.mid & pc.not_end)(self.down_mid.start)

    def down(self):
        pc = self.pc
        pl.when(jnp.logical_not(pc.mid))(self.cross_c.wait_recv)
        pl.when(jnp.logical_not(pc.mid) & pc.not_end)(self.down_far.start)

    def result(self, write):
        pc = self.pc
        pl.when(pc.mid)(lambda: write(self.zt))
        pl.when(jnp.logical_not(pc.mid))(lambda: write(self.zi))

    def drain(self):
        pc = self.pc
        pl.when(pc.mid)(self.cross_c.wait_send)
        pl.when(jnp.logical_not(pc.mid))(self.up_c.wait_send)
        pl.when(pc.mid & pc.not_end)(self.down_mid.wait_send)
        pl.when(jnp.logical_not(pc.mid) & pc.not_end)(self.down_far.wait_send)


class Scatter:
    def __init__(self, pc, part, width, l0, la, lb, la2, lb2, ssem, rsem, then=None):
        self.pc, self.part, self.l0, self.then = pc, part, l0, then
        self.la, self.lb, self.la2, self.lb2 = la, lb, la2, lb2
        h = width // 2
        A, B = self.A, self.B = pl.ds(0, h), pl.ds(h, h)
        lead = (slice(None),) * (len(l0.shape) - 3)
        xb, yb = pc.xb, pc.yb

        def blk(y, x, cols):
            return l0.at[(y, x, *lead, cols)]

        self.blk = blk
        other = 1 - pc.core
        self.pair = [
            rcopy(part(2 * q + other), l0.at[q // 2, q % 2], ssem.at[q], rsem.at[q], pc.sib)
            for q in range(4)
        ]
        every = slice(None)
        self.first = [
            rcopy(blk(every, 1 - xb, A), la, ssem.at[4], rsem.at[4], pc.xn),
            rcopy(blk(1 - yb, every, B), lb, ssem.at[5], rsem.at[5], pc.yn),
        ]
        self.second = [
            rcopy(blk(1 - yb, xb, A), la2, ssem.at[6], rsem.at[6], pc.yn),
            rcopy(blk(yb, 1 - xb, B), lb2, ssem.at[7], rsem.at[7], pc.xn),
        ]

    def p0(self):
        for c in self.pair:
            c.start()

    def p1(self):
        for q in range(4):
            self.pair[q].wait_recv()
            own = self.part(2 * q + self.pc.core)[...]
            self.l0[q // 2, q % 2] = add(self.l0[q // 2, q % 2], own)
        for c in self.first:
            c.start()

    def into(self, y, x, cols, got):
        v = self.blk(y, x, cols)
        v[...] = add(v[...], got[...])

    def p2(self):
        xb, yb = self.pc.xb, self.pc.yb
        self.first[0].wait_recv()
        self.into(1 - yb, xb, self.A, self.la.at[1 - yb])
        self.second[0].start()
        self.first[1].wait_recv()
        self.into(yb, 1 - xb, self.B, self.lb.at[1 - xb])
        self.second[1].start()
        self.into(yb, xb, self.A, self.la.at[yb])
        self.into(yb, xb, self.B, self.lb.at[xb])

    def p3(self):
        for c, cols, got in zip(self.second, (self.A, self.B), (self.la2, self.lb2)):
            c.wait_recv()
            self.into(self.pc.yb, self.pc.xb, cols, got)
        self.then()

    def drain(self):
        for c in self.pair + self.first + self.second:
            c.wait_send()


class Job:
    def __init__(self, scatter, line, out, sem):
        self.scatter, self.line = scatter, line
        scatter.then = line.send
        self.p0, self.p1, self.p2, self.p3 = scatter.p0, scatter.p1, scatter.p2, scatter.p3
        self.up, self.mid, self.dn = line.up, line.middle, line.down
        self.out, self.sem = out, sem

    def store(self):
        self.line.result(lambda src: pltpu.make_async_copy(src, self.out, self.sem).start())

    def drain(self):
        pltpu.make_async_copy(self.line.zo, self.out, self.sem).wait()
        self.scatter.drain()
        self.line.drain()


class Vectors:
    def __init__(self, pc, vec, tot, land, ssem, rsem, line):
        self.vec, self.tot, self.land, self.line = vec, tot, land, line
        self.steps = [
            rcopy(tot.at[k], land.at[k], ssem.at[k], rsem.at[k], peer)
            for k, peer in enumerate((pc.sib, pc.xn, pc.yn))
        ]
        self.up, self.mid, self.dn = line.up, line.middle, line.down

    def p0(self):
        self.tot[0] = jnp.sum(self.vec[...], axis=1)
        self.steps[0].start()

    def take(self, k):
        self.steps[k].wait_recv()
        self.tot[k + 1] = self.tot[k] + self.land[k]

    def p1(self):
        self.take(0)
        self.steps[1].start()

    def p2(self):
        self.take(1)
        self.steps[2].start()

    def p3(self):
        self.take(2)
        self.line.send()

    def drain(self):
        for c in self.steps:
            c.wait_send()
        self.line.drain()


def scatter_scratch(lead, width):
    half = width // 2
    return dict(
        l0=pltpu.VMEM((2, 2, *lead, width), bf16),
        la=pltpu.VMEM((2, *lead, half), bf16),
        lb=pltpu.VMEM((2, *lead, half), bf16),
        la2=pltpu.VMEM((*lead, half), bf16),
        lb2=pltpu.VMEM((*lead, half), bf16),
        ssem=pltpu.SemaphoreType.DMA((8,)),
        rsem=pltpu.SemaphoreType.DMA((8,)),
    )


def line_scratch(shape, kind):
    return dict(
        zo=pltpu.VMEM(shape, kind),
        zi=pltpu.VMEM(shape, kind),
        ssem=pltpu.SemaphoreType.DMA((3,)),
        rsem=pltpu.SemaphoreType.DMA((2,)),
    )


class Gather:
    def __init__(self, pc, kv, rows, ssem, rsem):
        def blk(t, cols=slice(None)):
            return kv.at[rows, pl.ds(pl.multiple_of(t * 32, 32), 32), cols]

        h = kv.shape[-1] // 2
        A, B = pl.ds(0, h), pl.ds(h, h)
        ds_ = 2 * pc.dc + pc.core

        def copy(k, ref, peer):
            return rcopy(ref, ref, ssem.at[k], rsem.at[k], peer)

        self.own = [copy(0, blk(pc.s), pc.sib), copy(1, blk(pc.s), pc.xn), copy(2, blk(pc.s), pc.yn)]
        self.from_x = [copy(3, blk(pc.xn[0], A), pc.yn), copy(4, blk(pc.xn[0]), pc.sib)]
        self.from_y = [copy(5, blk(pc.yn[0], B), pc.xn), copy(6, blk(pc.yn[0]), pc.sib)]
        self.from_d = [copy(7, blk(ds_, A), pc.sib), copy(8, blk(ds_, B), pc.sib)]

    def p0(self):
        for c in self.own[::-1]:
            c.start()

    def p1(self):
        self.own[1].wait_recv()
        for c in self.from_x:
            c.start()
        self.own[2].wait_recv()
        for c in self.from_y:
            c.start()

    def p2(self):
        self.from_x[0].wait_recv()
        self.from_d[0].start()
        self.from_y[0].wait_recv()
        self.from_d[1].start()

    def p3(self):
        for c in (self.own[0], self.from_x[1], self.from_y[1], *self.from_d):
            c.wait_recv()

    def drain(self):
        for c in self.own + self.from_x + self.from_y + self.from_d:
            c.wait_send()


def kernel(n_rows, names, *refs):
    R = types.SimpleNamespace(**dict(zip(names, refs, strict=True)))
    q_hbm, c_hbm, lat_hbm = R.queries, R.cotangent, R.latents
    line_of = lambda ref: ref[...].reshape(1, -1)
    q_ref, c_ref, lat_ref = R.q_v, R.c_v, R.lat_v
    wq, wk, wv, wo, wu, wd = R.wq_v, R.wk_v, R.wv_v, R.wo_v, R.wu_v, R.wd_v
    kv, qn_s, qp_s, p_s, mix_s, hn_s = R.kv, R.qn, R.qp, R.p, R.mix, R.hn
    act_s, dpre_s, dres_s, dm_s, dq_s = R.act, R.dpre, R.dres, R.dm, R.dq
    s_scr, ds_scr, inv_s = R.s_scr, R.ds_scr, R.inv
    lidT, ln_s, dkv_own, vec = R.lidT, R.ln, R.dkv_own, R.vec
    rows, positions, width = q_ref.shape
    lats, lwidth = lat_ref.shape[1:]
    pair = 2
    n_pairs = rows // pair
    tokens = rows * positions
    span = positions * pair

    loads = {}
    for k, (name, src, dst) in enumerate(
        [
            ("lat", lat_hbm, lat_ref),
            ("wk", R.key_weight, wk),
            ("wv", R.value_weight, wv),
            ("q", q_hbm, q_ref),
            ("wq", R.query_weight, wq),
            ("wo", R.out_weight, wo),
            ("wu", R.up_weight, wu),
            ("wd", R.down_weight, wd),
            ("c", c_hbm, c_ref),
        ]
    ):
        loads[name] = pltpu.make_async_copy(src, dst, R.load_sem.at[k])
        loads[name].start()

    pc = Place(n_rows)
    pc.greet()

    def loop(first, last, body):
        def step(i, carry):
            body(i)
            return carry

        lax.fori_loop(first, last, step, 0)

    lane1 = lax.broadcasted_iota(jnp.int32, (1, 128), 1)

    def head_mask(hh, kind):
        return ((lane1 >= QKDIM * hh) & (lane1 < QKDIM * (hh + 1))).astype(kind)

    own = pl.ds(pl.multiple_of(pc.s * lats, lats), lats)

    def l0(g):
        rs = pl.ds(g * pair, pair)
        hat, _ = norm(flat(lat_ref[rs]).astype(f32))
        ln = (hat * line_of(R.gain_latent) + line_of(R.shift_latent)).astype(bf16)
        ln_s[pl.ds(g * pair * lats, pair * lats), :] = ln
        k = dg(ln, wk[...], 1, 0).astype(bf16)
        v = dg(ln, wv[...], 1, 0).astype(bf16)
        kv[rs, own, 0:256] = k.reshape(pair, lats, -1)
        kv[rs, own, 256:1024] = v.reshape(pair, lats, -1)

    def at(i):
        return pl.ds(pl.multiple_of(i * span, span), span)

    def row(r):
        return pl.ds(pl.multiple_of(r * positions, positions), positions)

    def f1(i):
        hat, _ = norm(flat(q_ref[pl.ds(i * pair, pair)]).astype(f32))
        qn = (hat * line_of(R.gain_query) + line_of(R.shift_query)).astype(bf16)
        qn_s[at(i), :] = qn
        qp_s[at(i), :] = (dg(qn, wq[...], 1, 0) * SCALE).astype(bf16)

    def f1b(i):
        c = flat(c_ref[pl.ds(i * pair, pair)])
        vec[5, :, :width] += row_sum(c.astype(f32))
        dpre_s[at(i), :] = dg(c, wd[...], 1, 1).astype(bf16)

    def row8(r):
        return pl.ds(pl.multiple_of(r * HEADS * 256, HEADS * 256), HEADS * 256)

    def f2(r):
        k = kv[r, :, :256]
        vT = kv[r, :, 256:].T
        lane = lax.broadcasted_iota(jnp.int32, (256, 128), 1)
        col = jnp.sum(jnp.where(lane == r, lidT[...], 0.0), axis=1, keepdims=True)
        allowed = col == R.query_ids[pl.ds(r, 1), :].astype(f32)
        for g in range(2):
            kb = k[:, 128 * g : 128 * g + 128]
            km = jnp.concatenate([kb * head_mask(hh, bf16) for hh in range(4)], axis=0)
            sg = dg(km, qp_s[row(r), 128 * g : 128 * g + 128], 1, 1)
            for hh in range(4):
                s_scr[4 * g + hh] = sg[256 * hh : 256 * (hh + 1)]
        p_r = p_s.at[row8(r)]
        for h in range(HEADS):
            s = jnp.where(allowed, s_scr[h], -1e30)
            e = jnp.exp(s - jnp.max(s, axis=0, keepdims=True))
            p_r[256 * h : 256 * (h + 1), :] = e.astype(bf16)
            inv_s[r, h : h + 1, :] = 1.0 / jnp.sum(e, axis=0, keepdims=True)
        mix_r = mix_s.at[:, row(r)]
        for h in range(HEADS):
            hs = slice(HDIM * h, HDIM * (h + 1))
            got = dg(vT[hs], p_r[256 * h : 256 * (h + 1), :], 1, 0)
            mix_r[hs, :] = (got * inv_s[r, h : h + 1, :]).astype(bf16)

    def chunks(dst, sems, i, n):
        return [
            pltpu.make_async_copy(
                ds_scr.at[pl.ds(k * n, n)],
                dst.at[pl.ds(pl.multiple_of(i * n, n), n), pl.ds(256 * k, 256)],
                sems.at[k],
            )
            for k in range(width // 256)
        ]

    def stage(value, dst, sems, i, n):
        for k, c in enumerate(chunks(dst, sems, i, n)):
            ds_scr[n * k : n * (k + 1), :] = value[:, 256 * k : 256 * (k + 1)].astype(bf16)
            c.start()

    def staged(dst, sems, i, n):
        for c in chunks(dst, sems, i, n):
            c.wait()

    def f3(i, between):
        rs = pl.ds(i * pair, pair)
        resid = flat(q_ref[rs]).astype(f32) + dg(mix_s[:, at(i)], wo[...], 0, 0)
        hat, inv = norm(resid)
        hn = (hat * line_of(R.gain_hidden) + line_of(R.shift_hidden)).astype(bf16)
        hn_s[at(i), :] = hn
        pre = dg(hn, wu[...], 1, 0) + line_of(R.bias_up)
        phi = 0.5 * (1.0 + lax.erf(pre * (0.5**0.5)))
        act = (pre * phi).astype(bf16)
        act_s[at(i), :] = act
        slope = phi + pre * (jnp.exp(-0.5 * pre * pre) * 0.3989422804014327)
        dpre = (dpre_s[at(i), :].astype(f32) * slope).astype(bf16)
        dpre_s[at(i), :] = dpre

        between()
        out = resid + dg(act, wd[...], 1, 0) + line_of(R.bias_down)
        stage(out, R.block_out, R.bo_sem, i, span)
        vec[4, :, :width] += row_sum(dpre.astype(f32))
        dh = dg(dpre, wu[...], 1, 1)
        vec[2, :, :width] += row_sum(dh * hat)
        vec[3, :, :width] += row_sum(dh)
        cf = flat(c_ref[rs]).astype(f32)
        dlow = (norm_back(dh, line_of(R.gain_hidden), hat, inv) + cf).astype(bf16)
        dres_s[at(i), :] = dlow
        dm_s[:, at(i)] = dg(wo[...], dlow, 1, 1).astype(bf16)
        staged(R.block_out, R.bo_sem, i, span)

    def b2(r):
        k = kv[r, :, :256]
        kT = k.T
        v = kv[r, :, 256:]
        dvs, dqs, dks = [], [], []
        p_r, dm_r, qp_r = p_s.at[row8(r)], dm_s.at[:, row(r)], qp_s.at[row(r)]
        for h in range(HEADS):
            hs = slice(HDIM * h, HDIM * (h + 1))
            dm_r[hs, :] = (dm_r[hs, :].astype(f32) * inv_s[r, h : h + 1, :]).astype(bf16)
        for h in range(HEADS):
            hs = slice(HDIM * h, HDIM * (h + 1))
            s_scr[h] = dg(v[:, hs], dm_r[hs, :], 1, 0)
        for h in range(HEADS):
            hs = slice(HDIM * h, HDIM * (h + 1))
            dvs.append(dg(dm_r[hs, :], p_r[256 * h : 256 * (h + 1), :], 1, 1).astype(bf16))
        for h in range(HEADS):
            e = p_r[256 * h : 256 * (h + 1), :].astype(f32)
            ed = e * s_scr[h]
            ds = ed - e * (jnp.sum(ed, axis=0, keepdims=True) * inv_s[r, h : h + 1, :])
            ds_scr[256 * h : 256 * (h + 1), :] = ds.astype(bf16)
        for g in range(2):
            t = dg(ds_scr[1024 * g : 1024 * (g + 1), :], qp_r[:, 128 * g : 128 * g + 128], 1, 0)
            dks.append(sum(t[256 * hh : 256 * (hh + 1)] * head_mask(hh, f32) for hh in range(4)))
        for h in range(HEADS):
            kh = kT[QKDIM * h : QKDIM * (h + 1)]
            dqs.append(dg(kh, ds_scr[256 * h : 256 * (h + 1), :], 1, 0).astype(bf16))
        dq_s[row(r), :] = jnp.concatenate(dqs, axis=0).T
        kv[r, :, :128] = dks[0].astype(bf16)
        kv[r, :, 128:256] = dks[1].astype(bf16)
        kv[r, :, 256:] = jnp.concatenate(dvs, axis=0).T

    def b3(r):
        dqn = dg(dq_s[row(r), :], wq[...], 1, 1) * SCALE
        hat, inv = norm(q_ref[r].astype(f32))
        vec[0, :, :width] += row_sum(dqn * hat)
        vec[1, :, :width] += row_sum(dqn)

        got = norm_back(dqn, line_of(R.gain_query), hat, inv) + dres_s[row(r), :].astype(f32)

        if r >= 1:
            staged(R.grad_queries, R.gq_sem, r - 1, positions)

        stage(got, R.grad_queries, R.gq_sem, r, positions)

    def cols(j):
        return pl.ds(pl.multiple_of(j * 256, 256), 256)

    def cols_at(j):
        return pl.ds(256 * j, 256)

    def w_down(j):
        R.g_down[:, cols_at(j)] = dg(act_s[...], flat(c_ref[:, :, cols_at(j)]), 0, 0).astype(bf16)

    g_up, g_out = act_s.at[pl.ds(0, width)], hn_s.at[pl.ds(0, width)]

    def w_up(j):
        g_up[:, cols_at(j)] = dg(hn_s[...], dpre_s[:, cols_at(j)], 0, 0).astype(bf16)

    def w_out(j):
        g_out[:, cols_at(j)] = dg(mix_s[...], dres_s[:, cols_at(j)], 1, 0).astype(bf16)

    def w_q():
        R.g_q[...] = (dg(qn_s[...], dq_s[...], 0, 0) * SCALE).astype(bf16)

    def w_kv(j):
        got = dg(ln_s[:, cols(j)], dkv_own[...], 0, 0).astype(bf16)
        for k in range(4):
            to = pl.ds(pl.multiple_of(k * lwidth + j * 256, 256), 256)
            p_s[to, :] = got[:, 256 * k : 256 * (k + 1)]

    put_gl = [
        pltpu.make_async_copy(
            ds_scr.at[pl.ds(1024 + k * rows * lats, rows * lats)], R.grad_latents.at[:, pl.ds(256 * k, 256)], R.gl_sem.at[k]
        )
        for k in range(lwidth // 256)
    ]

    def l1():
        d = dg(dkv_own[:, :256], wk[...], 1, 1) + dg(dkv_own[:, 256:], wv[...], 1, 1)
        hat, inv = norm(flat(lat_ref[...]).astype(f32))
        vec[6] += row_sum(d * hat)
        vec[7] += row_sum(d)
        got = norm_back(d, line_of(R.gain_latent), hat, inv)
        for k, c in enumerate(put_gl):
            ds_scr[1024 + k * rows * lats : 1024 + (k + 1) * rows * lats, :] = got[:, 256 * k : 256 * (k + 1)].astype(bf16)
            c.start()

    G = [Gather(pc, kv, pl.ds(g * pair, pair), R.ag_s.at[g], R.ag_r.at[g]) for g in range(n_pairs)]

    def job(k, ref, lo, c0, height, out):
        block = height // 8

        def part(t):
            return ref.at[pl.ds(pl.multiple_of(lo + t * block, 32), block), pl.ds(c0, 256)]

        sc = R.sc[k]
        ln = Line(pc, sc["l0"].at[pc.yb, pc.xb], kind=bf16, **R.li[k])
        return Job(Scatter(pc, part, 256, **sc), ln, out, R.t_sem.at[k])

    D = [job(j, R.g_down, 0, 256 * j, width, R.t_down.at[:, cols_at(j)]) for j in range(3)]
    U = [job(3 + j, act_s, 0, 256 * j, width, R.t_up.at[:, cols_at(j)]) for j in range(3)]
    O = [job(6 + j, hn_s, 0, 256 * j, width, R.t_out.at[:, cols_at(j)]) for j in range(3)]
    Q = job(9, R.g_q, 0, 0, width, R.t_q)
    K = [job(10 + j, p_s, j * lwidth, 0, lwidth, R.t_kv.at[j]) for j in range(4)]

    def keys_values(g):
        def part(t):
            return kv.at[pl.ds(g * pair, pair), pl.ds(pl.multiple_of(t * lats, lats), lats), :]

        sc = R.scd[g]

        def keep():
            dkv_own[pl.ds(g * pair * lats, pair * lats), :] = flat(sc["l0"][pc.yb, pc.xb])

        return Scatter(pc, part, 1024, then=keep, **sc)

    DKV = [keys_values(g) for g in range(n_pairs)]
    lv = Line(pc, R.vtot.at[3], kind=f32, **R.ln_vec)
    V = Vectors(pc, vec, R.vtot, R.vland, R.vs, R.vr, lv)

    vec[...] = jnp.zeros_like(vec)
    lid = R.latent_ids[...].astype(f32)
    lidT[...] = jnp.concatenate([lid, jnp.zeros((128 - rows, lid.shape[1]), f32)], axis=0).T
    loads["lat"].wait()
    loads["wk"].wait()
    loads["wv"].wait()
    l0(0)
    pc.met()
    G[0].p0()
    loads["q"].wait()
    loads["wq"].wait()
    f1(0)
    l0(1)
    G[1].p0()
    f1(1)
    f1(2)
    l0(2)
    G[0].p1()
    G[2].p0()
    loads["c"].wait()
    loads["wd"].wait()
    f1b(0)
    f1b(1)
    f1b(2)
    G[1].p1()
    G[0].p2()
    G[0].p3()
    loads["wo"].wait()
    loads["wu"].wait()
    hooks = {
        0: {
            2: (DKV[0].p3,),
        },
        1: {
            0: (G[2].p1,),
            1: (DKV[0].p1,),
            2: (DKV[1].p1,),
        },
        2: {
            0: (G[1].p2,),
        },
        3: {
            0: (G[2].p2, G[1].p3, G[0].drain,),
            1: (DKV[0].p2, G[1].drain,),
            2: (DKV[1].p2, G[2].drain,),
        },
        4: {
            0: (G[2].p3,),
        },
        5: {
            0: (DKV[0].p0,),
            1: (DKV[1].p0,),
            2: (DKV[2].p0,),
        },
    }

    def hook(k, i):
        for p, fns in hooks.get(k, {}).items():

            @pl.when(i == p)
            def _():
                for fn in fns:
                    fn()

    def main(i):
        f2(pair * i)
        hook(0, i)
        f2(pair * i + 1)
        hook(1, i)
        f3(i, lambda: hook(2, i))
        hook(3, i)
        b2(pair * i)
        hook(4, i)
        b2(pair * i + 1)
        hook(5, i)

    loop(0, n_pairs, main)
    w_down(0)
    DKV[1].p3()
    D[0].p0()
    w_down(1)
    DKV[2].p1()
    D[0].p1()
    D[1].p0()
    w_down(2)
    D[2].p0()
    w_up(0)
    D[1].p1()
    U[0].p0()
    D[2].p1()
    w_up(1)
    U[0].p1()
    U[1].p0()
    w_up(2)
    DKV[2].p2()
    U[1].p1()
    U[2].p0()
    w_out(0)
    D[0].p2()
    O[0].p0()
    D[1].p2()
    U[2].p1()
    D[2].p2()
    O[0].p1()
    U[0].p2()
    DKV[2].p3()
    loop(0, 5, w_kv)
    U[1].p2()
    D[0].p3()
    K[0].p0()
    K[1].p0()
    K[2].p0()
    K[3].p0()
    D[1].p3()
    l1()
    U[2].p2()
    K[0].p1()
    D[2].p3()
    K[1].p1()
    b3(0)
    K[2].p1()
    O[0].p2()
    D[0].up()
    U[0].p3()
    K[3].p1()
    U[1].p3()
    b3(1)
    D[1].up()
    U[2].p3()
    b3(2)
    D[2].up()
    b3(3)
    K[0].p2()
    D[0].mid()
    U[0].up()
    b3(4)
    K[1].p2()
    U[1].up()
    D[1].mid()
    b3(5)
    U[2].up()
    D[2].mid()
    V.p0()
    w_q()
    K[2].p2()
    O[0].p3()
    D[0].dn()
    V.p1()
    U[0].mid()
    U[1].mid()
    D[1].dn()
    K[3].p2()
    Q.p0()
    w_out(1)
    U[2].mid()
    K[0].p3()
    D[2].dn()
    O[1].p0()
    Q.p1()
    K[1].p3()
    w_out(2)
    K[2].p3()
    O[1].p1()
    O[0].up()
    U[0].dn()
    O[2].p0()
    V.p2()
    U[1].dn()
    K[3].p3()
    O[2].p1()
    U[2].dn()
    K[0].up()
    Q.p2()
    O[1].p2()
    O[0].mid()
    K[1].up()
    V.p3()
    O[2].p2()
    K[2].up()
    Q.p3()
    O[1].p3()
    K[0].mid()
    O[0].dn()
    K[3].up()
    K[1].mid()
    O[2].p3()
    V.up()
    Q.up()
    K[2].mid()
    O[1].up()
    K[0].dn()
    K[3].mid()
    O[2].up()
    K[1].dn()
    V.mid()
    Q.mid()
    K[2].dn()
    O[1].mid()
    O[2].mid()
    K[3].dn()
    V.dn()
    Q.dn()
    O[1].dn()
    O[2].dn()
    jobs = [*D, *U, *O, Q, *K]
    for x in jobs:
        x.store()
    t_vec = pltpu.make_async_copy(lv.zo, R.t_vec, R.t_sem.at[len(jobs)])
    lv.result(lambda src: pltpu.make_async_copy(src, R.t_vec, R.t_sem.at[len(jobs)]).start())
    for x in (*jobs, *DKV, V):
        x.drain()
    t_vec.wait()
    staged(R.grad_queries, R.gq_sem, rows - 1, positions)
    for c in put_gl:
        c.wait()


def unpack(*refs):
    n = len(Outs._fields)
    ins, out = refs[:9], Outs(*refs[9 : 9 + n])
    stay, wide, narrow = refs[9 + n : 18 + n], refs[18 + n : -3], refs[-3]
    sem_in, sem_out = refs[-2], refs[-1]
    loads = [pltpu.make_async_copy(a, b, sem_in.at[k]) for k, (a, b) in enumerate(zip(ins, stay))]
    for c in loads:
        c.start()
    t_vec = stay[8]
    outs = (
        out.block_out,
        out.grad_queries,
        out.grad_latents,
        out.grad_down_weight,
        out.grad_up_weight,
        out.grad_out_weight,
        out.grad_query_weight,
        out.grad_key_weight,
        out.grad_value_weight,
    )
    stores = [pltpu.make_async_copy(stay[0], out.block_out, sem_out.at[0])]
    stores += [pltpu.make_async_copy(v, outs[k + 1], sem_out.at[k + 1]) for k, v in enumerate(wide)]
    loads[1].wait()
    half = wide[0].shape[0] // 2
    halves = []
    for j in range(2):
        rs = pl.ds(j * half, half)
        wide[0][rs] = stay[1][rs].astype(f32)
        halves.append(pltpu.make_async_copy(wide[0].at[rs], out.grad_queries.at[rs], narrow.at[j]))
        halves[-1].start()
    stores = stores[:1] + stores[2:]
    loads[0].wait()
    stores[0].start()
    for k in range(1, 6):
        loads[k + 1].wait()
        wide[k][...] = stay[k + 1][...].astype(f32)
        stores[k].start()
    loads[7].wait()
    wide[6][...] = stay[7][0].astype(f32)
    stores[6].start()
    for k in range(3):
        wide[7][:, 256 * k : 256 * (k + 1)] = stay[7][k + 1].astype(f32)
    stores[7].start()
    loads[8].wait()
    vectors = (
        out.grad_gain_query,
        out.grad_shift_query,
        out.grad_gain_hidden,
        out.grad_shift_hidden,
        out.grad_bias_up,
        out.grad_bias_down,
        out.grad_gain_latent,
        out.grad_shift_latent,
    )
    for t in range(8):

        @pl.when(lax.axis_index("seq") == t)
        def _():
            for k, ref in enumerate(vectors):
                m = ref.shape[0]
                ref[...] = t_vec[k, m * t : m * (t + 1)]

    for c in stores + halves:
        c.wait()


class Args(NamedTuple):
    queries: Any
    latents: Any
    query_ids: Any
    latent_ids: Any
    query_weight: Any
    key_weight: Any
    value_weight: Any
    out_weight: Any
    up_weight: Any
    down_weight: Any
    gain_query: Any
    shift_query: Any
    gain_latent: Any
    shift_latent: Any
    gain_hidden: Any
    shift_hidden: Any
    bias_up: Any
    bias_down: Any
    cotangent: Any


class Outs(NamedTuple):
    block_out: Any
    grad_queries: Any
    grad_latents: Any
    grad_query_weight: Any
    grad_key_weight: Any
    grad_value_weight: Any
    grad_out_weight: Any
    grad_up_weight: Any
    grad_down_weight: Any
    grad_gain_query: Any
    grad_shift_query: Any
    grad_gain_latent: Any
    grad_shift_latent: Any
    grad_gain_hidden: Any
    grad_shift_hidden: Any
    grad_bias_up: Any
    grad_bias_down: Any


def body(n_rows, n_seq, *args):
    A = Args(*args)
    rows, pos, width = A.queries.shape
    lats, lwidth = A.latents.shape[1:]
    nl = lats * n_seq
    F_ = lambda *s: jax.ShapeDtypeStruct(s, f32)
    wide, vec, lvec = F_(width // n_seq, width), F_(width // n_seq), F_(lwidth // n_seq)
    out = Outs(
        block_out=jax.ShapeDtypeStruct((rows, pos, width), bf16),
        grad_queries=F_(rows, pos, width),
        grad_latents=F_(rows, lats, lwidth),
        grad_query_weight=F_(width // n_seq, 256),
        grad_key_weight=F_(lwidth // n_seq, 256),
        grad_value_weight=F_(lwidth // n_seq, width),
        grad_out_weight=wide,
        grad_up_weight=wide,
        grad_down_weight=wide,
        grad_gain_query=vec,
        grad_shift_query=vec,
        grad_gain_latent=lvec,
        grad_shift_latent=lvec,
        grad_gain_hidden=vec,
        grad_shift_hidden=vec,
        grad_bias_up=vec,
        grad_bias_down=vec,
    )
    V = lambda *s: pltpu.VMEM(s, bf16)
    F = lambda *s: pltpu.VMEM(s, f32)
    dma = lambda *s: pltpu.SemaphoreType.DMA(s)
    tok = V(rows, pos, width)
    tok2 = V(rows * pos, width)
    tokT = V(width, rows * pos)
    scratch = dict(
        q_v=tok,
        c_v=tok,
        lat_v=V(rows, lats, lwidth),
        wq_v=V(width, 256),
        wk_v=V(lwidth, 256),
        wv_v=V(lwidth, width),
        wo_v=V(width, width),
        wu_v=V(width, width),
        wd_v=V(width, width),
        kv=V(rows, nl, 1024),
        qn=tok2,
        qp=V(rows * pos, 256),
        s_scr=F(HEADS, nl, pos),
        ds_scr=V(HEADS * nl, pos),
        inv=F(rows, HEADS, pos),
        p=V(rows * HEADS * nl, pos),
        mix=tokT,
        hn=tok2,
        act=tok2,
        dpre=tok2,
        dres=tok2,
        dm=tokT,
        dq=V(rows * pos, 256),
        lidT=F(nl, 128),
        ln=V(rows * lats, lwidth),
        dkv_own=V(rows * lats, 1024),
        vec=F(8, 8, lwidth),
        vtot=F(4, 8, lwidth),
        vland=F(3, 8, lwidth),
        vs=dma(3),
        vr=dma(3),
        bo_sem=dma(width // 256),
        gq_sem=dma(width // 256),
        gl_sem=dma(lwidth // 256),
        t_sem=dma(15),
        load_sem=dma(9),
        ag_s=dma(rows // 2, 9),
        ag_r=dma(rows // 2, 9),
        g_down=V(width, width),
        g_q=V(width, 256),
        ln_vec=line_scratch((8, lwidth), f32),
    )
    lead, llead = (width // n_seq,), (lwidth // n_seq,)
    shapes = [lead] * 10 + [llead] * 4
    scratch["sc"] = [scatter_scratch(x, 256) for x in shapes]
    scratch["li"] = [line_scratch((*x, 256), bf16) for x in shapes]
    scratch["scd"] = [scatter_scratch((2, lats), 1024) for _ in range(rows // 2)]
    any_ = pl.BlockSpec(memory_space=pl.ANY)
    vm = pl.BlockSpec(memory_space=pltpu.VMEM)
    far = (A.queries, A.cotangent, A.latents, *A[4:10])
    in_specs = [any_ if any(a is f for f in far) else vm for a in A]
    sds = jax.ShapeDtypeStruct
    mid = dict(
        block_out=sds((rows * pos, width), bf16),
        grad_queries=sds((rows * pos, width), bf16),
        grad_latents=sds((rows * lats, lwidth), bf16),
        t_down=sds(wide.shape, bf16),
        t_up=sds(wide.shape, bf16),
        t_out=sds(wide.shape, bf16),
        t_q=sds((width // n_seq, 256), bf16),
        t_kv=sds((4, lwidth // n_seq, 256), bf16),
        t_vec=sds((8, lwidth), f32),
    )
    names = (*Args._fields, *mid, *scratch)
    flops = 2 * rows * pos * width * width * 14
    got = pl.pallas_call(
        functools.partial(kernel, n_rows, names),
        out_shape=tuple(mid.values()),
        in_specs=in_specs,
        out_specs=(any_,) * len(mid),
        scratch_shapes=list(scratch.values()),
        compiler_params=pltpu.CompilerParams(
            collective_id=0, has_side_effects=True, vmem_limit_bytes=64 << 20
        ),
        cost_estimate=pl.CostEstimate(flops=flops, bytes_accessed=24 << 20, transcendentals=0),
    )(*A)
    three = lambda x: x.reshape(rows, -1, x.shape[-1])
    got = (three(got[0]), three(got[1]), three(got[2]), *got[3:])
    return pl.pallas_call(
        unpack,
        out_shape=tuple(out),
        in_specs=[any_] * 9,
        out_specs=(any_,) * 9 + (vm,) * 8,
        scratch_shapes=[pltpu.VMEM(x.shape, x.dtype) for x in got]
        + [
            pltpu.VMEM(o.shape, f32)
            for o in (
                out.grad_queries,
                out.grad_latents,
                wide,
                wide,
                wide,
                out.grad_query_weight,
                out.grad_key_weight,
                out.grad_value_weight,
            )
        ]
        + [dma(2), dma(9), dma(9)],
        compiler_params=pltpu.CompilerParams(vmem_limit_bytes=64 << 20),
        cost_estimate=pl.CostEstimate(flops=0, bytes_accessed=18 << 20, transcendentals=0),
    )(*got)


def solution(mesh):
    seq = P("rows", "seq", None)
    rep = P()
    in_specs = (seq, seq, P("rows", "seq"), P("rows", None)) + (rep,) * 14 + (seq,)
    out_specs = (seq,) * 3 + (P("seq", None),) * 6 + (P("seq"),) * 8
    return jax.shard_map(
        functools.partial(body, mesh.shape["rows"], mesh.shape["seq"]),
        mesh=mesh,
        in_specs=in_specs,
        out_specs=out_specs,
        check_vma=False,
    )
```

time: 128 us -> 113 us (0.88)
  Pallas kernels: 127 us -> 112 us
    pallas_call x1, Pallas kernels: 118 us -> 105 us  [body(): pl.pallas_call(functools.partial(kernel, n_rows, names), out_shape=tuple(...]
    pallas_call x1, Pallas kernels: 8.97 us -> 6.99 us  [body(): pl.pallas_call(unpack, out_shape=tuple(out), in_specs=[any_] * 9, out_spe...]
where the time goes in v2:
time: 113 us
  Pallas kernels  112 us (99%)
    pallas_call x1, Pallas kernels, body(): pl.pallas_call(functools.partial(kernel, n_rows, names), out_shape=tuple(...  105 us
    pallas_call x1, Pallas kernels, body(): pl.pallas_call(unpack, out_shape=tuple(out), in_specs=[any_] * 9, out_spe...  6.99 us

profile of v2, /device:TPU:0, one launch (start us, length us, event | category | flops | bytes accessed | tf_op | source)
XLA Modules:
  0.0 112.9 jit_solution(2578903213437599937)
XLA Ops:
  0.7 105.0 %shard_map.314 = (bf16[1536,768]{1,0:T(8,128)(2,1)}, bf16[1536,768]{1,0:T(8,128)(2,1)}, bf16[192,1280]{1,0:T(8,128)(2,1)}, bf16[96,768]{1,0:T(8,128)(2,1)}, bf16...) custom-call(bf16[6,256,768]{2,1,0:T(8,128)(2,1)} %refs_0_.1, ...), custom_call_target="tpu_custom_call" | custom-call | flops 25367150592 | bytes 25165824 | tf_op jit(solution)/shard_map/pallas_call | solution.py:1024
  105.7 7.0 %shard_map.315 = (bf16[6,256,768]{2,1,0:T(8,128)(2,1)}, f32[6,256,768]{2,1,0:T(8,128)}, f32[6,32,1280]{2,1,0:T(8,128)}, f32[96,256]{1,0:T(8,128)}, f32[160,256]{...) custom-call(bf16[6,256,768]{2,1,0:T(8,128)(2,1)} %bitcast.3, ...), custom_call_target="tpu_custom_call" | custom-call | bytes 18874368 | tf_op jit(solution)/shard_map/pallas_call | solution.py:1037

commit v3 on v2

--- a/solution.py
+++ b/solution.py
@@ -451,7 +451,7 @@
         for c in chunks(dst, sems, i, n):
             c.wait()
 
-    def f3(i, between):
+    def f3(i):
         rs = pl.ds(i * pair, pair)
         resid = flat(q_ref[rs]).astype(f32) + dg(mix_s[:, at(i)], wo[...], 0, 0)
         hat, inv = norm(resid)
@@ -465,7 +465,6 @@
         dpre = (dpre_s[at(i), :].astype(f32) * slope).astype(bf16)
         dpre_s[at(i), :] = dpre
 
-        between()
         out = resid + dg(act, wd[...], 1, 0) + line_of(R.bias_down)
         stage(out, R.block_out, R.bo_sem, i, span)
         vec[4, :, :width] += row_sum(dpre.astype(f32))
@@ -628,27 +627,37 @@
     loads["wo"].wait()
     loads["wu"].wait()
     hooks = {
-        0: {
-            2: (DKV[0].p3,),
-        },
         1: {
-            0: (G[2].p1,),
+            0: (
+                G[2].p1,
+                G[1].p2,
+            ),
             1: (DKV[0].p1,),
-            2: (DKV[1].p1,),
-        },
-        2: {
-            0: (G[1].p2,),
+            2: (
+                DKV[0].p3,
+                DKV[1].p1,
+            ),
         },
         3: {
-            0: (G[2].p2, G[1].p3, G[0].drain,),
-            1: (DKV[0].p2, G[1].drain,),
-            2: (DKV[1].p2, G[2].drain,),
-        },
-        4: {
-            0: (G[2].p3,),
+            0: (
+                G[2].p2,
+                G[1].p3,
+                G[0].drain,
+            ),
+            1: (
+                DKV[0].p2,
+                G[1].drain,
+            ),
+            2: (
+                DKV[1].p2,
+                G[2].drain,
+            ),
         },
         5: {
-            0: (DKV[0].p0,),
+            0: (
+                G[2].p3,
+                DKV[0].p0,
+            ),
             1: (DKV[1].p0,),
             2: (DKV[2].p0,),
         },
@@ -664,13 +673,11 @@
 
     def main(i):
         f2(pair * i)
-        hook(0, i)
         f2(pair * i + 1)
         hook(1, i)
-        f3(i, lambda: hook(2, i))
+        f3(i)
         hook(3, i)
         b2(pair * i)
-        hook(4, i)
         b2(pair * i + 1)
         hook(5, i)
 

time: 113 us -> 111 us (0.982)
  Pallas kernels: 112 us -> 110 us
    pallas_call x1, Pallas kernels: 105 us -> 103 us  [body(): pl.pallas_call(functools.partial(kernel, n_rows, names), out_shape=tuple(...]
where the time goes in v3:
time: 111 us
  Pallas kernels  110 us (99%)
    pallas_call x1, Pallas kernels, body(): pl.pallas_call(functools.partial(kernel, n_rows, names), out_shape=tuple(...  103 us
    pallas_call x1, Pallas kernels, body(): pl.pallas_call(unpack, out_shape=tuple(out), in_specs=[any_] * 9, out_spe...  6.99 us

profile of v3, /device:TPU:0, one launch (start us, length us, event | category | flops | bytes accessed | tf_op | source)
XLA Modules:
  0.0 110.8 jit_solution(12408018830995842441)
XLA Ops:
  0.7 102.9 %shard_map.314 = (bf16[1536,768]{1,0:T(8,128)(2,1)}, bf16[1536,768]{1,0:T(8,128)(2,1)}, bf16[192,1280]{1,0:T(8,128)(2,1)}, bf16[96,768]{1,0:T(8,128)(2,1)}, bf16...) custom-call(bf16[6,256,768]{2,1,0:T(8,128)(2,1)} %refs_0_.1, ...), custom_call_target="tpu_custom_call" | custom-call | flops 25367150592 | bytes 25165824 | tf_op jit(solution)/shard_map/pallas_call | solution.py:1031
  103.6 7.0 %shard_map.315 = (bf16[6,256,768]{2,1,0:T(8,128)(2,1)}, f32[6,256,768]{2,1,0:T(8,128)}, f32[6,32,1280]{2,1,0:T(8,128)}, f32[96,256]{1,0:T(8,128)}, f32[160,256]{...) custom-call(bf16[6,256,768]{2,1,0:T(8,128)(2,1)} %bitcast.3, ...), custom_call_target="tpu_custom_call" | custom-call | bytes 18874368 | tf_op jit(solution)/shard_map/pallas_call | solution.py:1044

commit v4 on v3

--- a/solution.py
+++ b/solution.py
@@ -710,6 +710,10 @@
     D[2].p2()
     O[0].p1()
     U[0].p2()
+    w_out(1)
+    O[1].p0()
+    w_out(2)
+    O[2].p0()
     DKV[2].p3()
     loop(0, 5, w_kv)
     U[1].p2()
@@ -724,12 +728,17 @@
     K[0].p1()
     D[2].p3()
     K[1].p1()
+    w_q()
+    Q.p0()
     b3(0)
     K[2].p1()
     O[0].p2()
     D[0].up()
     U[0].p3()
     K[3].p1()
+    O[1].p1()
+    O[2].p1()
+    Q.p1()
     U[1].p3()
     b3(1)
     D[1].up()
@@ -748,7 +757,6 @@
     U[2].up()
     D[2].mid()
     V.p0()
-    w_q()
     K[2].p2()
     O[0].p3()
     D[0].dn()
@@ -757,32 +765,24 @@
     U[1].mid()
     D[1].dn()
     K[3].p2()
-    Q.p0()
-    w_out(1)
+    O[1].p2()
+    O[2].p2()
+    Q.p2()
     U[2].mid()
     K[0].p3()
     D[2].dn()
-    O[1].p0()
-    Q.p1()
     K[1].p3()
-    w_out(2)
     K[2].p3()
-    O[1].p1()
     O[0].up()
     U[0].dn()
-    O[2].p0()
     V.p2()
     U[1].dn()
     K[3].p3()
-    O[2].p1()
     U[2].dn()
     K[0].up()
-    Q.p2()
-    O[1].p2()
     O[0].mid()
     K[1].up()
     V.p3()
-    O[2].p2()
     K[2].up()
     Q.p3()
     O[1].p3()

time: 111 us -> 113 us (1.018)
  Pallas kernels: 110 us -> 112 us
    pallas_call x1, Pallas kernels: 103 us -> 105 us  [body(): pl.pallas_call(functools.partial(kernel, n_rows, names), out_shape=tuple(...]
where the time goes in v4:
time: 113 us
  Pallas kernels  112 us (99%)
    pallas_call x1, Pallas kernels, body(): pl.pallas_call(functools.partial(kernel, n_rows, names), out_shape=tuple(...  105 us
    pallas_call x1, Pallas kernels, body(): pl.pallas_call(unpack, out_shape=tuple(out), in_specs=[any_] * 9, out_spe...  6.99 us

profile of v4, /device:TPU:0, one launch (start us, length us, event | category | flops | bytes accessed | tf_op | source)
XLA Modules:
  0.0 113.1 jit_solution(8920899523294984998)
XLA Ops:
  0.7 105.2 %shard_map.314 = (bf16[1536,768]{1,0:T(8,128)(2,1)}, bf16[1536,768]{1,0:T(8,128)(2,1)}, bf16[192,1280]{1,0:T(8,128)(2,1)}, bf16[96,768]{1,0:T(8,128)(2,1)}, bf16...) custom-call(bf16[6,256,768]{2,1,0:T(8,128)(2,1)} %refs_0_.1, ...), custom_call_target="tpu_custom_call" | custom-call | flops 25367150592 | bytes 25165824 | tf_op jit(solution)/shard_map/pallas_call | solution.py:1031
  105.9 7.0 %shard_map.315 = (bf16[6,256,768]{2,1,0:T(8,128)(2,1)}, f32[6,256,768]{2,1,0:T(8,128)}, f32[6,32,1280]{2,1,0:T(8,128)}, f32[96,256]{1,0:T(8,128)}, f32[160,256]{...) custom-call(bf16[6,256,768]{2,1,0:T(8,128)(2,1)} %bitcast.3, ...), custom_call_target="tpu_custom_call" | custom-call | bytes 18874368 | tf_op jit(solution)/shard_map/pallas_call | solution.py:1044
